TPU v7x, 512 devices: a whole 4x8x8 slice. The times are simulated.
512 devices in a mesh: rows: 128 (over z, y, core), ingest: 4 (over x).
Axes of the slice: x: 4, y: 8, z: 8, core: 2. Of those that a mesh axis runs over, the one named last changes fastest.
Arguments:
- covariates: float32 [64, 4194304], P(None, ('rows', 'ingest')), may hold values from -6 to 6
- intervals: int32 [4194304], P(('rows', 'ingest')), may hold values from 0 to 4
- offsets: float32 [4194304], P(('rows', 'ingest')), may hold values from 0 to 1
- responses: float32 [4194304], P(('rows', 'ingest')), may hold values from -6 to 6
- counts: int32 [512], P(('rows', 'ingest')), may hold values from 1 to 8192, 2097152 in all
- smoothing: float32 [64], replicated, may hold values from 0.01 to 1
Outputs:
- factor: float32 [512, 512], replicated
- projected: float32 [512], replicated
Inputs may be any that keep to these rules, and one draw needn't show every extreme that they name: A device's live rows are its first counts slots; the counts sum to 2097152 and one device is full.
All inputs are finite; a program needn't handle non-finite values.
Results may differ from a plain program's by a relative error of at most 0.0003.
Values sent between devices are 32-bit elements; how exact they have to be, the bound alone decides.
No kernel may reach another device: no remote copies, remote signals or barrier semaphores. Data moves between devices by JAX's collectives and lax.ppermute only.
A program may use at most 128 MiB of HBM per device.

v0:
```python
import math

import jax
import jax.numpy as jnp
from jax import lax
from jax.sharding import PartitionSpec as P

P_COV = 64
N_BASIS = 8


def spline_values(intervals, offsets):
    first = (1.0 - offsets) ** 3 / 6.0
    second = (3.0 * offsets**3 - 6.0 * offsets**2 + 4.0) / 6.0
    third = (-3.0 * offsets**3 + 3.0 * offsets**2 + 3.0 * offsets + 1.0) / 6.0
    fourth = offsets**3 / 6.0
    basis_ids = jnp.arange(N_BASIS, dtype=jnp.int32)[:, None]
    result = jnp.where(intervals[None, :] == basis_ids, first[None, :], 0.0)
    result = result + jnp.where(intervals[None, :] + 1 == basis_ids, second[None, :], 0.0)
    result = result + jnp.where(intervals[None, :] + 2 == basis_ids, third[None, :], 0.0)
    result = result + jnp.where(intervals[None, :] + 3 == basis_ids, fourth[None, :], 0.0)
    return result


def penalty(smoothing):
    identity = jnp.eye(N_BASIS, dtype=jnp.float32)
    second = identity[:-2] - 2.0 * identity[1:-1] + identity[2:]
    kernel = jnp.dot(
        second.T, second, precision=lax.Precision.HIGHEST, preferred_element_type=jnp.float32
    )
    same_cov = jnp.eye(P_COV, dtype=jnp.float32)
    blocks = same_cov[:, None, :, None] * smoothing[:, None, None, None] * kernel[None, :, None, :]
    width = P_COV * N_BASIS
    return blocks.reshape(width, width)


def accumulate(packed_rows, live_count):
    slots = packed_rows.shape[1]
    width = P_COV * N_BASIS
    block_rows = min(512, slots)
    blocks = slots // block_rows

    def block_step(block_index, state_pair):

        def add_block(pair):
            row_block = lax.dynamic_slice_in_dim(
                packed_rows, block_index * block_rows, block_rows, 1
            )
            basis = row_block[P_COV : P_COV + N_BASIS]
            design = (row_block[:P_COV][:, None, :] * basis[None, :, :]).reshape(width, block_rows)
            design = design * row_block[P_COV + N_BASIS + 1][None, :]
            gram_part = lax.dot_general(
                design,
                design,
                (((1,), (1,)), ((), ())),
                precision=lax.Precision.HIGHEST,
                preferred_element_type=jnp.float32,
            )
            moment_part = jnp.dot(
                design,
                row_block[P_COV + N_BASIS],
                precision=lax.Precision.HIGHEST,
                preferred_element_type=jnp.float32,
            )
            return (pair[0] + gram_part, pair[1] + moment_part)

        return lax.cond(
            block_index * block_rows < live_count, add_block, lambda pair: pair, state_pair
        )

    start_pair = (jnp.zeros((width, width), jnp.float32), jnp.zeros((width,), jnp.float32))
    return lax.fori_loop(0, blocks, block_step, start_pair)


def combine(summands):
    partial_sums = lax.psum((summands[0], summands[1]), "ingest")
    return lax.psum((partial_sums[0], partial_sums[1]), "rows")


def per_device(covariates, intervals, offsets, responses, counts, smoothing):
    slots = covariates.shape[1]
    live_count = counts[0]
    slot_ids = jnp.arange(slots, dtype=jnp.int32)
    live_mask = (slot_ids < live_count).astype(jnp.float32)
    basis = spline_values(intervals, offsets)
    packed_rows = jnp.concatenate(
        [covariates, basis, responses[None, :], live_mask[None, :]], axis=0
    )
    gram_matrix, moment = accumulate(packed_rows, live_count)
    gram_matrix, moment = combine((gram_matrix, moment))
    total_live = lax.axis_size("rows") * lax.axis_size("ingest") * slots // 2
    gram_matrix = gram_matrix / total_live + penalty(smoothing)
    moment = moment / math.sqrt(total_live)
    lower_factor = jnp.linalg.cholesky(gram_matrix)
    projected = lax.linalg.triangular_solve(
        lower_factor, moment[:, None], left_side=True, lower=True
    )[:, 0]
    return (lower_factor.T, projected)


def solution(mesh):
    return jax.shard_map(
        per_device,
        mesh=mesh,
        in_specs=(
            P(None, ("rows", "ingest")),
            P(("rows", "ingest")),
            P(("rows", "ingest")),
            P(("rows", "ingest")),
            P(("rows", "ingest")),
            P(),
        ),
        out_specs=(P(), P()),
        check_vma=False,
    )
```

profile of v0, /device:TPU:1, one launch (start us, length us, event | category | flops | bytes accessed | tf_op | source)
XLA Modules:
  0.0 612.1 jit_solution(10612082358084056705)
XLA Ops:
  10.3 3.3 pad_maximum_fusion
  13.8 61.6 %while.16 = (s32[]{:T(128)}, f32[512,512]{1,0:T(8,128)S(1)}, f32[512]{0:T(512)S(1)}, s32[]{:T(128)}, f32[74,8192]{1,0:T(8,128)}, /*index=5*/s32[]{:T(128)}, s32[]{:T(128)}) while((s32[]{:T(128)}, f32[512,512]{1,0:T(8,128)S(1)}, f32[512]{0:T(512)S(1)}, s32[]{:T(128)}, f32[74,8192]{1,0:T(8,128)}, /*index=5*/s32[]{:T(128)}, s32[]{:T(128)}) %tuple.75), condition=%wide.region_3.4_spmd, body=%wide.region_0.3_spmd.sunk | while | flops 1615069696 | bytes 2705693 | solution.py:72
  14.5 6.3 %conditional.2 = ((f32[512,512]{1,0:T(8,128)S(1)}, f32[512]{0:T(512)S(1)})) conditional(s32[]{:T(128)} %convert_element_type.29, (f32[512,512]{1,0:T(8,128)S(1)}, f32[512]{0:T(512)S(1)}) %tuple.69, (s32[]{:T(128)}, f32[74,8192]{1,0:T(8,128)}, f32[512,512]{1,0:T(8,128)S(1)}, f32[512]{0:T(512)S(1)}) %tuple.70), branch_computations={%region_1.1_spmd, %region_2.2_spmd} | conditional | flops 1615069696 | bytes 2705534 | solution.py:67
  21.5 6.3 %conditional.2 = ((f32[512,512]{1,0:T(8,128)S(1)}, f32[512]{0:T(512)S(1)})) conditional(s32[]{:T(128)} %convert_element_type.29, (f32[512,512]{1,0:T(8,128)S(1)}, f32[512]{0:T(512)S(1)}) %tuple.69, (s32[]{:T(128)}, f32[74,8192]{1,0:T(8,128)}, f32[512,512]{1,0:T(8,128)S(1)}, f32[512]{0:T(512)S(1)}) %tuple.70), branch_computations={%region_1.1_spmd, %region_2.2_spmd} | conditional | flops 1615069696 | bytes 2705534 | solution.py:67
  28.5 6.3 %conditional.2 = ((f32[512,512]{1,0:T(8,128)S(1)}, f32[512]{0:T(512)S(1)})) conditional(s32[]{:T(128)} %convert_element_type.29, (f32[512,512]{1,0:T(8,128)S(1)}, f32[512]{0:T(512)S(1)}) %tuple.69, (s32[]{:T(128)}, f32[74,8192]{1,0:T(8,128)}, f32[512,512]{1,0:T(8,128)S(1)}, f32[512]{0:T(512)S(1)}) %tuple.70), branch_computations={%region_1.1_spmd, %region_2.2_spmd} | conditional | flops 1615069696 | bytes 2705534 | solution.py:67
  35.5 6.3 %conditional.2 = ((f32[512,512]{1,0:T(8,128)S(1)}, f32[512]{0:T(512)S(1)})) conditional(s32[]{:T(128)} %convert_element_type.29, (f32[512,512]{1,0:T(8,128)S(1)}, f32[512]{0:T(512)S(1)}) %tuple.69, (s32[]{:T(128)}, f32[74,8192]{1,0:T(8,128)}, f32[512,512]{1,0:T(8,128)S(1)}, f32[512]{0:T(512)S(1)}) %tuple.70), branch_computations={%region_1.1_spmd, %region_2.2_spmd} | conditional | flops 1615069696 | bytes 2705534 | solution.py:67
  42.5 6.3 %conditional.2 = ((f32[512,512]{1,0:T(8,128)S(1)}, f32[512]{0:T(512)S(1)})) conditional(s32[]{:T(128)} %convert_element_type.29, (f32[512,512]{1,0:T(8,128)S(1)}, f32[512]{0:T(512)S(1)}) %tuple.69, (s32[]{:T(128)}, f32[74,8192]{1,0:T(8,128)}, f32[512,512]{1,0:T(8,128)S(1)}, f32[512]{0:T(512)S(1)}) %tuple.70), branch_computations={%region_1.1_spmd, %region_2.2_spmd} | conditional | flops 1615069696 | bytes 2705534 | solution.py:67
  49.6 6.3 %conditional.2 = ((f32[512,512]{1,0:T(8,128)S(1)}, f32[512]{0:T(512)S(1)})) conditional(s32[]{:T(128)} %convert_element_type.29, (f32[512,512]{1,0:T(8,128)S(1)}, f32[512]{0:T(512)S(1)}) %tuple.69, (s32[]{:T(128)}, f32[74,8192]{1,0:T(8,128)}, f32[512,512]{1,0:T(8,128)S(1)}, f32[512]{0:T(512)S(1)}) %tuple.70), branch_computations={%region_1.1_spmd, %region_2.2_spmd} | conditional | flops 1615069696 | bytes 2705534 | solution.py:67
  56.6 6.3 %conditional.2 = ((f32[512,512]{1,0:T(8,128)S(1)}, f32[512]{0:T(512)S(1)})) conditional(s32[]{:T(128)} %convert_element_type.29, (f32[512,512]{1,0:T(8,128)S(1)}, f32[512]{0:T(512)S(1)}) %tuple.69, (s32[]{:T(128)}, f32[74,8192]{1,0:T(8,128)}, f32[512,512]{1,0:T(8,128)S(1)}, f32[512]{0:T(512)S(1)}) %tuple.70), branch_computations={%region_1.1_spmd, %region_2.2_spmd} | conditional | flops 1615069696 | bytes 2705534 | solution.py:67
  63.6 6.3 %conditional.2 = ((f32[512,512]{1,0:T(8,128)S(1)}, f32[512]{0:T(512)S(1)})) conditional(s32[]{:T(128)} %convert_element_type.29, (f32[512,512]{1,0:T(8,128)S(1)}, f32[512]{0:T(512)S(1)}) %tuple.69, (s32[]{:T(128)}, f32[74,8192]{1,0:T(8,128)}, f32[512,512]{1,0:T(8,128)S(1)}, f32[512]{0:T(512)S(1)}) %tuple.70), branch_computations={%region_1.1_spmd, %region_2.2_spmd} | conditional | flops 1615069696 | bytes 2705534 | solution.py:67
  77.1 111.1 %all-reduce.4.cloned.1.call-done = f32[512,512]{0,1:T(8,128)} async-done(((f32[512,512]{0,1:T(8,128)}), f32[512,512]{0,1:T(8,128)}) %all-reduce.4.cloned.1.call-update) | async-done | bytes 1048592 | tf_op jit(solution)/shard_map/psum | solution.py:76
  188.2 7.9 %broadcast_multiply_fusion = f32[64,8,64,8]{3,2,1,0:T(8,128)} fusion(f32[8,8]{1,0:T(8,128)S(1)} %fusion.42, f32[64,64]{1,0:T(8,128)S(1)} %fusion.40), kind=kLoop, calls=%fused_computation.15 | loop fusion | flops 262144 | bytes 1065216 | tf_op jit(solution)/shard_map/mul | solution.py:32
  196.2 12.6 %mul.132 = f32[512,512]{1,0:T(8,128)S(1)} reshape(f32[64,8,64,8]{3,2,1,0:T(8,128)} %broadcast_multiply_fusion) | data formatting | bytes 2097152 | tf_op jit(solution)/shard_map/mul | solution.py:32
  209.1 7.8 %psum.30 = f32[512]{0:T(512)S(1)} all-reduce(f32[512]{0:T(512)S(1)} %get-tuple-element.120), channel_id=1, replica_groups=mesh['rows'=128,'ingest'=4] {'ingest'}, use_global_device_ids=true, to_apply=%region_14.15 | all-reduce | flops 512 | bytes 4096 | tf_op jit(solution)/shard_map/psum | solution.py:76
  217.0 251.6 %psum.31 = f32[512]{0:T(512)S(1)} all-reduce(f32[512]{0:T(512)S(1)} %psum.30), channel_id=1, replica_groups=mesh['rows'=128,'ingest'=4] {'rows'}, use_global_device_ids=true, to_apply=%region_15.16 | all-reduce | flops 512 | bytes 4096 | tf_op jit(solution)/shard_map/psum | solution.py:77
  470.6 11.7 %cholesky.103 = f32[128,128]{1,0:T(8,128)S(1)} custom-call(f32[128,128]{1,0:T(8,128)S(1)} %cholesky.263), custom_call_target="Cholesky" | custom-call | tf_op jit(solution)/shard_map/jit(cholesky)/cholesky | solution.py:94
  482.5 9.8 %custom-call.30 = f32[1,128,128]{1,2,0:T(8,128)S(1)} custom-call(f32[1,128,128]{2,1,0:T(8,128)S(1)} %get-tuple-element.164), custom_call_target="InvertDiagBlocksLowerTriangular" | custom-call | tf_op jit(solution)/shard_map/jit(cholesky)/cholesky | solution.py:94
  493.0 11.7 %cholesky.215 = f32[128,128]{1,0:T(8,128)S(1)} custom-call(f32[128,128]{1,0:T(8,128)S(1)} %cholesky.267), custom_call_target="Cholesky" | custom-call | tf_op jit(solution)/shard_map/jit(cholesky)/cholesky | solution.py:94
  504.8 10.0 %custom-call.31 = f32[1,128,128]{1,2,0:T(8,128)S(1)} custom-call(f32[1,128,128]{2,1,0:T(8,128)S(1)} %get-tuple-element.161), custom_call_target="InvertDiagBlocksLowerTriangular" | custom-call | tf_op jit(solution)/shard_map/jit(cholesky)/cholesky | solution.py:94
  515.4 11.7 %cholesky.236 = f32[128,128]{1,0:T(8,128)S(1)} custom-call(f32[128,128]{1,0:T(8,128)S(1)} %cholesky.272), custom_call_target="Cholesky" | custom-call | tf_op jit(solution)/shard_map/jit(cholesky)/cholesky | solution.py:94
  527.2 9.8 %custom-call.32 = f32[1,128,128]{1,2,0:T(8,128)S(1)} custom-call(f32[1,128,128]{2,1,0:T(8,128)S(1)} %get-tuple-element.158), custom_call_target="InvertDiagBlocksLowerTriangular" | custom-call | tf_op jit(solution)/shard_map/jit(cholesky)/cholesky | solution.py:94
  537.6 11.7 %cholesky.253 = f32[128,128]{1,0:T(8,128)S(1)} custom-call(f32[128,128]{1,0:T(8,128)S(1)} %convolution_subtract_fusion.2), custom_call_target="Cholesky" | custom-call | tf_op jit(solution)/shard_map/jit(cholesky)/cholesky | solution.py:94
  555.7 8.1 %while.17 = (s32[]{:T(128)}, f32[512,512]{1,0:T(8,128)S(1)}, s32[4,2]{0,1:T(2,128)S(1)}, f32[4,128,128]{2,1,0:T(8,128)S(1)}, s32[]{:T(128)}) while((s32[]{:T(128)}, f32[512,512]{1,0:T(8,128)S(1)}, s32[4,2]{0,1:T(2,128)S(1)}, f32[4,128,128]{2,1,0:T(8,128)S(1)}, s32[]{:T(128)}) %tuple.78), condition=%wide.while_cond, body=%wide.while_body.sunk | while | flops 2 | bytes 131189 | solution.py:95
  563.9 39.3 %custom-call.33 = f32[4,128,128]{1,2,0:T(8,128)S(1)} custom-call(f32[4,128,128]{2,1,0:T(8,128)S(1)} %get-tuple-element.128), custom_call_target="InvertDiagBlocksLowerTriangular" | custom-call | tf_op jit(solution)/shard_map/triangular_solve | solution.py:95
  (120 shorter events, 73.4 us)
Async XLA Ops:
  7.2 181.1 %all-reduce.4.cloned.1.call-start = ((), (), s32[]{:S(2)}) async-start(), calls=%async_computation | async-start | bytes 2097152 | tf_op jit(solution)/shard_map/psum | solution.py:76
  75.5 1.6 copy-start
  76.8 391.8 %all-reduce.6.cloned.1.call-start = ((), (), s32[]{:S(2)}) async-start(), calls=%async_computation.1 | async-start | bytes 2097152 | tf_op jit(solution)/shard_map/psum | solution.py:77
Sparse Core Ops, SparseCore 0:
  76.9 111.2 all-reduce.3
  191.8 197.6 all-reduce.5
where the time goes:
time: 617 us; the launch traced here: 612 us
  blocking collectives  259 us (42%)
  other arithmetic  135 us (22%)
  waiting for transfers between devices  111 us (18%)
  local copies, waits for them, and re-layouts  43.6 us (7%)
  matrix products  34.5 us (6%)
  between operations  17.5 us (3%)
  loops' own time  11.2 us (2%)
    psum x1, blocking collectives, combine(): return lax.psum((partial_sums[0], partial_sums[1]), 'rows')  252 us
    psum x1, waiting for transfers between devices, combine(): partial_sums = lax.psum((summands[0], summands[1]), 'ingest')  111 us
    another operation x14, other arithmetic, per_device(): lower_factor = jnp.linalg.cholesky(gram_matrix)  78.9 us
    another operation x4, other arithmetic, per_device(): lax.linalg.triangular_solve(lower_factor, moment[:, None], left_side=True...  40.2 us
    dot_general x8, matrix products, add_block(): lax.dot_general(design, design, (((1,), (1,)), ((), ())), precision=lax.P...  16.8 us
    dot_general x8, matrix products, add_block(): jnp.dot(design, row_block[P_COV + N_BASIS], precision=lax.Precision.HIGHE...  14.1 us
    mul x2, local copies, waits for them, and re-layouts, penalty(): same_cov[:, None, :, None] * smoothing[:, None, None, None]  12.9 us
  transfers between devices with their start and end apart: 2, of which 1 were waited for; matrix products, arithmetic and copies ran while one was open for 3% of the time, Pallas kernels for 0%

commit v1 on v0

v1 whole, which is shorter than its diff:
```python
import math

import jax
import jax.numpy as jnp
import numpy as np
from jax import lax
from jax.experimental import pallas as pl
from jax.experimental.pallas import tpu as pltpu
from jax.sharding import Mesh, PartitionSpec as P

P_COV = 64
N_BASIS = 8
WIDTH = P_COV * N_BASIS
CHUNK = 2048
TOTAL_LIVE = 2097152
F32 = jnp.float32
BF16 = jnp.bfloat16
HIGHEST = lax.Precision.HIGHEST

PAIRS = [(j, k) for j in range(4) for k in range(j + 1)]
PAIRS += [(j, k) for j in range(4, 7) for k in range(1, 4) if j - k <= 3]
PAIRS += [(j, k) for j in range(4, 8) for k in range(4, j + 1)]
HALF = len(PAIRS) // 2
SHARES = 32
SHARE_ROWS = 16
SLAB_ROWS = SHARES * SHARE_ROWS
DIAG_ROW = 448
MOMENT_ROW = 464
NT = (((1,), (1,)), ((), ()))
TN = (((0,), (0,)), ((), ()))


def slab_place(pair_index):
    return (pair_index // 2) * P_COV, (pair_index % 2) * P_COV


def gram_kernel(count_ref, cov_ref, int_ref, off_ref, resp_ref, out_ref, hi_ref, lo_ref, hh_ref, lh_ref, mom_ref):
    step = pl.program_id(0)
    count = count_ref[0]

    @pl.when(step == 0)
    def _():
        hh_ref[...] = jnp.zeros_like(hh_ref)
        lh_ref[...] = jnp.zeros_like(lh_ref)
        mom_ref[...] = jnp.zeros_like(mom_ref)

    @pl.when(step * CHUNK < count)
    def _():
        cov = cov_ref[...]
        interval = int_ref[...]
        within = off_ref[...]
        slot = lax.broadcasted_iota(jnp.int32, (1, CHUNK), 1) + step * CHUNK
        live = jnp.where(slot < count, 1.0, 0.0).astype(F32)
        square = within * within
        cube = square * within
        rest = 1.0 - within
        first = rest * rest * rest * (1.0 / 6.0) * live
        second = (3.0 * cube - 6.0 * square + 4.0) * (1.0 / 6.0) * live
        third = (-3.0 * cube + 3.0 * square + 3.0 * within + 1.0) * (1.0 / 6.0) * live
        fourth = cube * (1.0 / 6.0) * live
        weights = []
        for j in range(N_BASIS):
            value = jnp.where(interval == j, first, 0.0)
            value = jnp.where(interval + 1 == j, second, value)
            value = jnp.where(interval + 2 == j, third, value)
            value = jnp.where(interval + 3 == j, fourth, value)
            weights.append(value)
            design = cov * value
            high = design.astype(BF16)
            hi_ref[j * P_COV : (j + 1) * P_COV, :] = high
            lo_ref[j * P_COV : (j + 1) * P_COV, :] = (design - high.astype(F32)).astype(BF16)
        cov_high = cov.astype(BF16)
        cov_low = (cov - cov_high.astype(F32)).astype(BF16)
        weighted = jnp.concatenate(weights, axis=0) * resp_ref[...]
        weighted_high = weighted.astype(BF16)
        weighted_low = (weighted - weighted_high.astype(F32)).astype(BF16)
        mom_ref[...] += lax.dot_general(
            jnp.concatenate([weighted_high, weighted_low], axis=0),
            jnp.concatenate([cov_high, cov_low], axis=0),
            NT,
            preferred_element_type=F32,
        )

        def product(left_ref, rows, columns):
            return lax.dot_general(left_ref[rows, :], hi_ref[columns, :], NT, preferred_element_type=F32)

        low, high_half = slice(0, 256), slice(256, 512)
        hh_ref[0:448, low] += product(hi_ref, slice(0, 448), low)
        lh_ref[0:448, low] += product(lo_ref, slice(0, 448), low)
        hh_ref[high_half, high_half] += product(hi_ref, high_half, high_half)
        lh_ref[64:512, high_half] += product(lo_ref, slice(64, 512), high_half)

    @pl.when(step == pl.num_programs(0) - 1)
    def _():
        row = lax.broadcasted_iota(jnp.int32, (P_COV, P_COV), 0)
        column = lax.broadcasted_iota(jnp.int32, (P_COV, P_COV), 1)

        def block(ref, j, k):
            return ref[j * P_COV : (j + 1) * P_COV, k * P_COV : (k + 1) * P_COV]

        def full(pair):
            j, k = pair
            return block(hh_ref, j, k) + block(lh_ref, j, k) + block(lh_ref, k, j).T

        out_ref[DIAG_ROW - 64 :, :] = jnp.zeros((SLAB_ROWS - DIAG_ROW + 64, 128), F32)
        for i in range(HALF):
            upper, lower = full(PAIRS[i]), full(PAIRS[HALF + i])
            r0, c0 = slab_place(i)
            out_ref[r0 : r0 + P_COV, c0 : c0 + P_COV] = jnp.where(row <= column, upper, lower)
            out_ref[DIAG_ROW + i : DIAG_ROW + i + 1, 0:P_COV] = jnp.sum(
                jnp.where(row == column, lower, 0.0), axis=0, keepdims=True
            )
        mom = mom_ref[...]
        out_ref[MOMENT_ROW : MOMENT_ROW + N_BASIS, 0:P_COV] = (
            mom[0:8, 0:P_COV] + mom[8:16, 0:P_COV] + mom[0:8, P_COV:]
        )


def local_sums(count, covariates, intervals, offsets, responses):
    slots = covariates.shape[1]
    per_row = pl.BlockSpec((1, CHUNK), lambda i: (0, i))
    return pl.pallas_call(
        gram_kernel,
        grid=(slots // CHUNK,),
        in_specs=[
            pl.BlockSpec(memory_space=pltpu.SMEM),
            pl.BlockSpec((P_COV, CHUNK), lambda i: (0, i)),
            per_row,
            per_row,
            per_row,
        ],
        out_specs=pl.BlockSpec((SLAB_ROWS, 128), lambda i: (0, 0)),
        out_shape=jax.ShapeDtypeStruct((SLAB_ROWS, 128), F32),
        scratch_shapes=[
            pltpu.VMEM((WIDTH, CHUNK), BF16),
            pltpu.VMEM((WIDTH, CHUNK), BF16),
            pltpu.VMEM((WIDTH, WIDTH), F32),
            pltpu.VMEM((WIDTH, WIDTH), F32),
            pltpu.VMEM((16, 128), F32),
        ],
        compiler_params=pltpu.CompilerParams(
            dimension_semantics=("arbitrary",), vmem_limit_bytes=40 * 1024 * 1024
        ),
        name="local_sums",
    )(count, covariates, intervals[None, :], offsets[None, :], responses[None, :])


def sum_repeat_kernel(parts, copies, in_ref, out_ref):
    rows = in_ref.shape[0] // parts
    total = in_ref[0:rows, :]
    for i in range(1, parts):
        total = total + in_ref[i * rows : (i + 1) * rows, :]
    for i in range(copies):
        out_ref[i * rows : (i + 1) * rows, :] = total


def sum_repeat(received, parts, copies):
    rows = received.shape[0] // parts
    return pl.pallas_call(
        lambda a, b: sum_repeat_kernel(parts, copies, a, b),
        out_shape=jax.ShapeDtypeStruct((copies * rows, 128), F32),
        name="sum_repeat",
    )(received)


def lane_spread(tile, lane):
    return jnp.broadcast_to(tile[:, lane : lane + 1], tile.shape)


def row_spread(tile, row):
    return jnp.broadcast_to(tile[row : row + 1, :], tile.shape)


def factor_tile(work, side):
    blocks = len(work)
    lanes = lax.broadcasted_iota(jnp.int32, (8, 128), 1)
    subs = lax.broadcasted_iota(jnp.int32, (8, 128), 0)
    factor_rows, inverse_rows = [], []
    for k in range(blocks):
        columns = [lane_spread(work[k], 8 * k + t) for t in range(8)]
        entry = {(s, t): row_spread(columns[t], s) for t in range(8) for s in range(t, 8)}
        rows = [row_spread(work[k], t) for t in range(8)]
        siderows = [row_spread(side[k], t) for t in range(8)]
        reciprocals, scale = [], {}
        for t in range(8):
            reciprocals.append(1.0 / entry[t, t])
            for s in range(t + 1, 8):
                scale[s, t] = entry[s, t] * reciprocals[t]
            for s in range(t + 1, 8):
                for u in range(t + 1, s + 1):
                    entry[s, u] = entry[s, u] - scale[s, t] * entry[u, t]
                rows[s] = rows[s] - scale[s, t] * rows[t]
                siderows[s] = siderows[s] - scale[s, t] * siderows[t]
        for b in range(k + 1, blocks):
            c = [lane_spread(work[b], 8 * k + t) for t in range(8)]
            for t in range(8):
                for s in range(t + 1, 8):
                    c[s] = c[s] - scale[s, t] * c[t]
                weight = c[t] * reciprocals[t]
                work[b] = work[b] - weight * rows[t]
                side[b] = side[b] - weight * siderows[t]
        out, sideout = jnp.zeros((8, 128), F32), jnp.zeros((8, 128), F32)
        for t in range(8):
            root = lax.rsqrt(entry[t, t])
            out = jnp.where(subs == t, rows[t] * root, out)
            sideout = jnp.where(subs == t, siderows[t] * root, sideout)
        factor_rows.append(jnp.where(lanes >= subs + 8 * k, out, 0.0))
        inverse_rows.append(jnp.where(lanes <= subs + 8 * k, sideout, 0.0))
    return factor_rows, inverse_rows


def factor_kernel(sums_ref, smooth_ref, factor_ref, proj_ref, half_ref, gram_ref, inv_ref):
    row = lax.broadcasted_iota(jnp.int32, (P_COV, P_COV), 0)
    column = lax.broadcasted_iota(jnp.int32, (P_COV, P_COV), 1)
    second = np.zeros((N_BASIS - 2, N_BASIS))
    for i in range(N_BASIS - 2):
        second[i, i : i + 3] = (1.0, -2.0, 1.0)
    penalty = second.T @ second
    smooth = jnp.where(row == column, smooth_ref[...], 0.0)
    pieces = {}

    def put(pair, value):
        j, k = pair
        value = value * (1.0 / TOTAL_LIVE)
        if penalty[j, k]:
            value = value + smooth * float(penalty[j, k])
        pieces[j, k] = pieces[k, j] = value

    for i in range(HALF):
        r0, c0 = slab_place(i)
        packed = sums_ref[r0 : r0 + P_COV, c0 : c0 + P_COV]
        turned = packed.T
        put(PAIRS[i], jnp.where(row <= column, packed, turned))
        diagonal = jnp.broadcast_to(sums_ref[DIAG_ROW + i : DIAG_ROW + i + 1, 0:P_COV], (P_COV, P_COV))
        lower = jnp.where(row > column, packed, turned)
        put(PAIRS[HALF + i], jnp.where(row == column, diagonal, lower))
    nothing = jnp.zeros((P_COV, P_COV), F32)
    for j in range(N_BASIS):
        for w in range(4):
            half_ref[w, pl.ds(j, P_COV, N_BASIS), :] = jnp.concatenate(
                [pieces.get((j, 2 * w), nothing), pieces.get((j, 2 * w + 1), nothing)], axis=1
            )
    for w in range(4):
        for i in range(4):
            turned = half_ref[w, 128 * i : 128 * i + 128, :].T
            for k in (2 * w, 2 * w + 1):
                gram_ref[i, pl.ds(k, P_COV, N_BASIS), :] = turned[(k - 2 * w) * P_COV : (k - 2 * w + 1) * P_COV, :]
    moment = sums_ref[MOMENT_ROW : MOMENT_ROW + N_BASIS, 0:P_COV].T * (1.0 / math.sqrt(TOTAL_LIVE))
    for j in range(N_BASIS):
        gram_ref[4, pl.ds(j, P_COV, N_BASIS), :] = jnp.broadcast_to(moment[:, j : j + 1], (P_COV, 128))

    factor_ref[...] = jnp.zeros_like(factor_ref)
    lanes = lax.broadcasted_iota(jnp.int32, (8, 128), 1)
    subs = lax.broadcasted_iota(jnp.int32, (8, 128), 0)

    def panel(p, _):
        start = pl.multiple_of(p * 128, 128)
        work = [gram_ref[p, pl.ds(pl.multiple_of(start + 8 * b, 8), 8), :] for b in range(16)]
        side = [jnp.where(lanes == subs + 8 * b, 1.0, 0.0).astype(F32) for b in range(16)]
        factor_rows, inverse_rows = factor_tile(work, side)
        for b in range(16):
            inv_ref[8 * b : 8 * b + 8, :] = inverse_rows[b]
            factor_ref[pl.ds(pl.multiple_of(start + 8 * b, 8), 8), pl.ds(start, 128)] = factor_rows[b]

        for q in range(4):

            @pl.when(p == q)
            def _():
                mine = slice(128 * q, 128 * q + 128)
                inverse = inv_ref[...]
                solved = {}
                for w in range(q + 1, 5):
                    solved[w] = jnp.dot(inverse, gram_ref[w, mine, :], precision=HIGHEST, preferred_element_type=F32)
                    gram_ref[w, mine, :] = solved[w]
                    if w < 4:
                        factor_ref[mine, 128 * w : 128 * w + 128] = solved[w]
                for i in range(q + 1, 4):
                    for w in range(i, 5):
                        gram_ref[w, 128 * i : 128 * i + 128, :] -= lax.dot_general(
                            solved[i], solved[w], TN, precision=HIGHEST, preferred_element_type=F32
                        )

        return 0

    lax.fori_loop(0, 4, panel, 0)
    diagonal_mask = lax.broadcasted_iota(jnp.int32, (128, 128), 0) == lax.broadcasted_iota(jnp.int32, (128, 128), 1)
    for p in range(4):
        tile = gram_ref[4, 128 * p : 128 * p + 128, :]
        proj_ref[:, 128 * p : 128 * p + 128] = jnp.sum(jnp.where(diagonal_mask, tile, 0.0), axis=0, keepdims=True)


def factorize(sums, smoothing):
    return pl.pallas_call(
        factor_kernel,
        out_shape=(
            jax.ShapeDtypeStruct((WIDTH, WIDTH), F32),
            jax.ShapeDtypeStruct((1, WIDTH), F32),
        ),
        scratch_shapes=[
            pltpu.VMEM((4, WIDTH, 128), F32),
            pltpu.VMEM((5, WIDTH, 128), F32),
            pltpu.VMEM((128, 128), F32),
        ],
        compiler_params=pltpu.CompilerParams(vmem_limit_bytes=40 * 1024 * 1024),
        name="factorize",
    )(sums, smoothing[None, :])


def per_device(covariates, intervals, offsets, responses, counts, smoothing):
    sums = local_sums(counts, covariates, intervals, offsets, responses)
    received = lax.all_to_all(sums.reshape(32, 16, 128), ("z", "x"), 0, 0, tiled=True)
    spread = sum_repeat(received.reshape(512, 128), 32, 16)
    received = lax.all_to_all(spread.reshape(16, 16, 128), ("y", "c"), 0, 0, tiled=True)
    spread = sum_repeat(received.reshape(256, 128), 16, 32)
    sums = lax.all_to_all(spread.reshape(32, 16, 128), ("z", "x"), 0, 0, tiled=True)
    factor, projected = factorize(sums.reshape(512, 128), smoothing)
    return factor, projected[0]


def solution(mesh):
    fine = Mesh(mesh.devices.reshape(8, 8, 2, 4), ("z", "y", "c", "x"))
    spread = ("z", "y", "c", "x")
    return jax.shard_map(
        per_device,
        mesh=fine,
        in_specs=(P(None, spread), P(spread), P(spread), P(spread), P(spread), P()),
        out_specs=(P(), P()),
        check_vma=False,
    )
```

time: 617 us -> 100 us (0.16)
  blocking collectives: 259 us -> 65.8 us
  other arithmetic: 135 us -> 0 us
  waiting for transfers between devices: 111 us -> 0 us
  local copies, waits for them, and re-layouts: 43.6 us -> 3.86 us
  matrix products: 34.5 us -> 0 us
  Pallas kernels: 0 us -> 28.8 us
  between operations: 17.5 us -> 1.3 us
  loops' own time: 11.2 us -> 0 us
    psum x2 -> x0, blocking collectives: 259 us -> none  [the longest x1 252 us: combine(): return lax.psum((partial_sums[0], partial_sums[1]), 'rows')]
    another operation x18 -> x0, other arithmetic: 119 us -> none  [the longest x14 78.9 us: per_device(): lower_factor = jnp.linalg.cholesky(gram_matrix)]
    psum x2 -> x0, waiting for transfers between devices: 111 us -> none  [the longest x1 111 us: combine(): partial_sums = lax.psum((summands[0], summands[1]), 'ingest')]
    all_to_all x0 -> x3, blocking collectives: none -> 65.8 us  [the longest x1 32.6 us: per_device(): lax.all_to_all(sums.reshape(32, 16, 128), ('z', 'x'), 0, 0, tiled=True)]
    dot_general x17 -> x0, matrix products: 31.2 us -> none  [the longest x8 16.8 us: add_block(): lax.dot_general(design, design, (((1,), (1,)), ((), ())), precision=lax.P...]
    pallas_call x0 -> x4, Pallas kernels: none -> 28.8 us  [the longest x1 21.2 us: factorize(): pl.pallas_call(factor_kernel, out_shape=(jax.ShapeDtypeStruct((WIDTH, WID...]
    slice x24 -> x0, local copies, waits for them, and re-layouts: 19.4 us -> none  [the longest x8 7.3 us: add_block(): row_block[:P_COV][:, None, :] * basis[None, :, :]]
    mul x2 -> x0, local copies, waits for them, and re-layouts: 12.9 us -> none  [penalty(): same_cov[:, None, :, None] * smoothing[:, None, None, None]]
  transfers between devices with their start and end apart: 2 -> 0, of which waited for: 1 -> 0; matrix products, arithmetic and copies ran while one was open for 3% -> 0% of each run, Pallas kernels for 0% -> 0%
where the time goes in v1:
time: 100 us; the launch traced here: 99.8 us
  blocking collectives  65.8 us (66%)
  Pallas kernels  28.8 us (29%)
  local copies, waits for them, and re-layouts  3.86 us (4%)
  between operations  1.3 us (1%)
    all_to_all x1, blocking collectives, per_device(): lax.all_to_all(sums.reshape(32, 16, 128), ('z', 'x'), 0, 0, tiled=True)  32.6 us
    pallas_call x1, Pallas kernels, factorize(): pl.pallas_call(factor_kernel, out_shape=(jax.ShapeDtypeStruct((WIDTH, WID...  21.2 us
    all_to_all x1, blocking collectives, per_device(): lax.all_to_all(spread.reshape(16, 16, 128), ('y', 'c'), 0, 0, tiled=True)  17.2 us
    all_to_all x1, blocking collectives, per_device(): lax.all_to_all(spread.reshape(32, 16, 128), ('z', 'x'), 0, 0, tiled=True)  16 us
    pallas_call x1, Pallas kernels, local_sums(): pl.pallas_call(gram_kernel, grid=(slots // CHUNK,), in_specs=[pl.BlockSpe...  4.29 us
    unnamed x10, local copies, waits for them, and re-layouts  3.86 us
    pallas_call x2, Pallas kernels, sum_repeat(): pl.pallas_call(lambda a, b: sum_repeat_kernel(parts, copies, a, b), out_s...  3.28 us

profile of v1, /device:TPU:1, one launch (start us, length us, event | category | flops | bytes accessed | tf_op | source)
XLA Modules:
  0.0 99.8 jit_solution(14142517606165882208)
XLA Ops:
  1.3 0.0 copy-start
  1.3 1.6 %copy-done = f32[64,8192]{1,0:T(8,128)S(1)} copy-done((f32[64,8192]{1,0:T(8,128)S(1)}, f32[64,8192]{1,0:T(8,128)}, u32[]{:S(2)}) %copy-start) | copy-done | bytes 2097176
  2.9 0.0 copy-start.1
  2.9 0.8 copy-done.1
  3.6 0.0 copy-start.2
  3.6 0.8 copy-done.2
  4.4 0.0 copy-start.3
  4.4 0.8 copy-done.3
  5.1 0.0 copy-start.4
  5.1 4.3 %local_sums.1 = f32[512,128]{1,0:T(8,128)S(1)} custom-call(s32[1]{0:T(128)S(6)} %copy.8.count_ref, f32[64,8192]{1,0:T(8,128)S(1)} %copy-done, s32[1,8192]{1,0:T(1,128)S(1)} %bitcast.13, f32[1,8192]{1,0:T(1,128)S(1)} %bitcast.14, f32[1,8192]{1,0:T(1,128)S(1)} %bitcast.15), custom_call_target="tpu_custom_call" | custom-call | tf_op jit(solution)/shard_map/local_sums/pallas_call | solution.py:122
  9.4 32.6 %all_to_all.15 = f32[32,16,128]{2,1,0:T(8,128)} all-to-all(f32[32,16,128]{2,1,0:T(8,128)S(1)} %bitcast.12), channel_id=1, replica_groups=mesh['z'=8,'y'=8,'c'=2,'x'=4] {'z','x'}, dimensions={0} | all-to-all | bytes 524288 | tf_op jit(solution)/shard_map/all_to_all | solution.py:311
  42.1 1.6 %sum_repeat.2 = f32[256,128]{1,0:T(8,128)} custom-call(f32[512,128]{1,0:T(8,128)} %bitcast.17), custom_call_target="tpu_custom_call" | custom-call | tf_op jit(solution)/shard_map/sum_repeat/pallas_call | solution.py:159
  43.7 17.2 %all_to_all.16 = f32[16,16,128]{2,1,0:T(8,128)} all-to-all(f32[16,16,128]{2,1,0:T(8,128)} %bitcast.19), channel_id=1, replica_groups=mesh['z'=8,'y'=8,'c'=2,'x'=4] {'y','c'}, dimensions={0} | all-to-all | bytes 262144 | tf_op jit(solution)/shard_map/all_to_all | solution.py:313
  60.9 1.6 %sum_repeat.3 = f32[512,128]{1,0:T(8,128)} custom-call(f32[256,128]{1,0:T(8,128)} %bitcast.20), custom_call_target="tpu_custom_call" | custom-call | tf_op jit(solution)/shard_map/sum_repeat/pallas_call | solution.py:159
  62.5 16.0 %all_to_all.17 = f32[32,16,128]{2,1,0:T(8,128)S(1)} all-to-all(f32[32,16,128]{2,1,0:T(8,128)} %bitcast.18), channel_id=1, replica_groups=mesh['z'=8,'y'=8,'c'=2,'x'=4] {'z','x'}, dimensions={0} | all-to-all | bytes 524288 | tf_op jit(solution)/shard_map/all_to_all | solution.py:315
  78.6 0.0 copy-done.4
  78.6 21.2 %factorize.1 = (f32[512,512]{1,0:T(8,128)}, f32[1,512]{1,0:T(1,128)}) custom-call(f32[512,128]{1,0:T(8,128)S(1)} %bitcast.11, f32[1,64]{1,0:T(1,128)S(1)} %bitcast.16), custom_call_target="tpu_custom_call" | custom-call | tf_op jit(solution)/shard_map/factorize/pallas_call | solution.py:293
Async XLA Ops:
  1.3 1.6 %copy-start = (f32[64,8192]{1,0:T(8,128)S(1)}, f32[64,8192]{1,0:T(8,128)}, u32[]{:S(2)}) copy-start(f32[64,8192]{1,0:T(8,128)} %cov_ref.1) | copy-start | bytes 6291460
  2.9 0.8 copy-start.1
  3.6 0.8 copy-start.2
  4.4 0.8 copy-start.3
  5.1 73.4 %copy-start.4 = (f32[64]{0:T(128)S(1)}, f32[64]{0:T(128)}, u32[]{:S(2)}) copy-start(f32[64]{0:T(128)} %param.11) | copy-start | bytes 772

commit v2 on v1

--- a/solution.py
+++ b/solution.py
@@ -11,45 +11,62 @@
 P_COV = 64
 N_BASIS = 8
 WIDTH = P_COV * N_BASIS
-CHUNK = 2048
+CHUNK = 1024
 TOTAL_LIVE = 2097152
 F32 = jnp.float32
 BF16 = jnp.bfloat16
 HIGHEST = lax.Precision.HIGHEST
 
-PAIRS = [(j, k) for j in range(4) for k in range(j + 1)]
-PAIRS += [(j, k) for j in range(4, 7) for k in range(1, 4) if j - k <= 3]
-PAIRS += [(j, k) for j in range(4, 8) for k in range(4, j + 1)]
-HALF = len(PAIRS) // 2
+ROW_SLABS = [(0, 0, 4), (0, 1, 1), (0, 2, 2), (0, 3, 3), (1, 2, 6), (1, 3, 3), (1, 4, 4), (1, 5, 5)]
+ROW_SLABS += [(2, 4, 4), (2, 5, 5), (2, 6, 6), (2, 7, 7), (3, 6, 6), (3, 7, 7)]
+HALF = len(ROW_SLABS) // 2
 SHARES = 32
 SHARE_ROWS = 16
 SLAB_ROWS = SHARES * SHARE_ROWS
-DIAG_ROW = 448
-MOMENT_ROW = 464
+DIAG_ROW = HALF * P_COV
+MOMENT_ROW = DIAG_ROW + 8
 NT = (((1,), (1,)), ((), ()))
 TN = (((0,), (0,)), ((), ()))
 
 
-def slab_place(pair_index):
-    return (pair_index // 2) * P_COV, (pair_index % 2) * P_COV
-
-
-def gram_kernel(count_ref, cov_ref, int_ref, off_ref, resp_ref, out_ref, hi_ref, lo_ref, hh_ref, lh_ref, mom_ref):
-    step = pl.program_id(0)
+def slab_masks():
+    row = lax.broadcasted_iota(jnp.int32, (P_COV, 128), 0)
+    column = lax.broadcasted_iota(jnp.int32, (P_COV, 128), 1)
+    return row, column % P_COV, column < P_COV
+
+
+def gram_kernel(
+    count_ref, cov_hbm, int_hbm, off_hbm, resp_hbm, out_ref,
+    cov_ref, int_ref, off_ref, resp_ref, hi_even, hi_odd, lo_even, lo_odd, hh_ref, lh_ref, mom_ref, row_sem, cov_sem,
+):
     count = count_ref[0]
-
-    @pl.when(step == 0)
-    def _():
-        hh_ref[...] = jnp.zeros_like(hh_ref)
-        lh_ref[...] = jnp.zeros_like(lh_ref)
-        mom_ref[...] = jnp.zeros_like(mom_ref)
-
-    @pl.when(step * CHUNK < count)
-    def _():
-        cov = cov_ref[...]
-        interval = int_ref[...]
-        within = off_ref[...]
-        slot = lax.broadcasted_iota(jnp.int32, (1, CHUNK), 1) + step * CHUNK
+    chunks = cov_hbm.shape[1] // CHUNK
+
+    def columns(c):
+        return pl.ds(pl.multiple_of(c * CHUNK, CHUNK), CHUNK)
+
+    row_copies = [
+        pltpu.make_async_copy(source, target, row_sem.at[i])
+        for i, (source, target) in enumerate([(int_hbm, int_ref), (off_hbm, off_ref), (resp_hbm, resp_ref)])
+    ]
+    cov_copies = [
+        pltpu.make_async_copy(cov_hbm.at[:, part], cov_ref.at[:, part], cov_sem.at[i])
+        for i, part in enumerate([slice(0, CHUNK), slice(CHUNK, chunks * CHUNK)])
+    ]
+    for copy in [*row_copies, *cov_copies]:
+        copy.start()
+    hh_ref[...] = jnp.zeros_like(hh_ref)
+    lh_ref[...] = jnp.zeros_like(lh_ref)
+    mom_ref[...] = jnp.zeros_like(mom_ref)
+    for copy in row_copies:
+        copy.wait()
+
+    def build(c, hi_ref, lo_ref):
+        part = columns(jnp.minimum(c, chunks - 1))
+        cov = cov_ref[:, part]
+        interval = int_ref[:, part]
+        within = off_ref[:, part]
+        slot = lax.broadcasted_iota(jnp.int32, (1, CHUNK), 1) + c * CHUNK
         live = jnp.where(slot < count, 1.0, 0.0).astype(F32)
         square = within * within
         cube = square * within
@@ -71,7 +88,7 @@
             lo_ref[j * P_COV : (j + 1) * P_COV, :] = (design - high.astype(F32)).astype(BF16)
         cov_high = cov.astype(BF16)
         cov_low = (cov - cov_high.astype(F32)).astype(BF16)
-        weighted = jnp.concatenate(weights, axis=0) * resp_ref[...]
+        weighted = jnp.concatenate(weights, axis=0) * resp_ref[:, part]
         weighted_high = weighted.astype(BF16)
         weighted_low = (weighted - weighted_high.astype(F32)).astype(BF16)
         mom_ref[...] += lax.dot_general(
@@ -81,6 +98,7 @@
             preferred_element_type=F32,
         )
 
+    def multiply(hi_ref, lo_ref):
         def product(left_ref, rows, columns):
             return lax.dot_general(left_ref[rows, :], hi_ref[columns, :], NT, preferred_element_type=F32)
 
@@ -90,57 +108,68 @@
         hh_ref[high_half, high_half] += product(hi_ref, high_half, high_half)
         lh_ref[64:512, high_half] += product(lo_ref, slice(64, 512), high_half)
 
-    @pl.when(step == pl.num_programs(0) - 1)
-    def _():
-        row = lax.broadcasted_iota(jnp.int32, (P_COV, P_COV), 0)
-        column = lax.broadcasted_iota(jnp.int32, (P_COV, P_COV), 1)
-
-        def block(ref, j, k):
-            return ref[j * P_COV : (j + 1) * P_COV, k * P_COV : (k + 1) * P_COV]
-
-        def full(pair):
-            j, k = pair
-            return block(hh_ref, j, k) + block(lh_ref, j, k) + block(lh_ref, k, j).T
-
-        out_ref[DIAG_ROW - 64 :, :] = jnp.zeros((SLAB_ROWS - DIAG_ROW + 64, 128), F32)
-        for i in range(HALF):
-            upper, lower = full(PAIRS[i]), full(PAIRS[HALF + i])
-            r0, c0 = slab_place(i)
-            out_ref[r0 : r0 + P_COV, c0 : c0 + P_COV] = jnp.where(row <= column, upper, lower)
-            out_ref[DIAG_ROW + i : DIAG_ROW + i + 1, 0:P_COV] = jnp.sum(
-                jnp.where(row == column, lower, 0.0), axis=0, keepdims=True
-            )
-        mom = mom_ref[...]
-        out_ref[MOMENT_ROW : MOMENT_ROW + N_BASIS, 0:P_COV] = (
-            mom[0:8, 0:P_COV] + mom[8:16, 0:P_COV] + mom[0:8, P_COV:]
+    cov_copies[0].wait()
+    build(0, hi_even, lo_even)
+    cov_copies[1].wait()
+
+    def pair(i, _):
+        build(2 * i + 1, hi_odd, lo_odd)
+        multiply(hi_even, lo_even)
+        build(2 * i + 2, hi_even, lo_even)
+        multiply(hi_odd, lo_odd)
+        return 0
+
+    lax.fori_loop(0, pl.cdiv(count, 2 * CHUNK), pair, 0)
+
+    row, column, left = slab_masks()
+    tiles = {}
+
+    def row_slab(entry):
+        w, j_left, j_right = entry
+        pieces = []
+        for j in (j_left, j_right):
+            t = j // 2
+            if (t, w) not in tiles:
+                at, across = slice(128 * t, 128 * t + 128), slice(128 * w, 128 * w + 128)
+                tiles[t, w] = hh_ref[at, across] + lh_ref[at, across] + lh_ref[across, at].T
+            pieces.append(tiles[t, w][(j % 2) * P_COV : (j % 2 + 1) * P_COV, :])
+        return pieces[0] if j_left == j_right else jnp.where(left, pieces[0], pieces[1])
+
+    out_ref[DIAG_ROW:, :] = jnp.zeros((SLAB_ROWS - DIAG_ROW, 128), F32)
+    for i in range(HALF):
+        upper, lower = row_slab(ROW_SLABS[i]), row_slab(ROW_SLABS[HALF + i])
+        out_ref[i * P_COV : (i + 1) * P_COV, :] = jnp.where(row <= column, upper, lower)
+        out_ref[DIAG_ROW + i : DIAG_ROW + i + 1, :] = jnp.sum(
+            jnp.where(row == column, lower, 0.0), axis=0, keepdims=True
         )
+    mom = mom_ref[...]
+    out_ref[MOMENT_ROW : MOMENT_ROW + N_BASIS, 0:P_COV] = mom[0:8, 0:P_COV] + mom[8:16, 0:P_COV] + mom[0:8, P_COV:]
 
 
 def local_sums(count, covariates, intervals, offsets, responses):
     slots = covariates.shape[1]
-    per_row = pl.BlockSpec((1, CHUNK), lambda i: (0, i))
+    in_place = pl.BlockSpec(memory_space=pltpu.HBM)
+    design = pltpu.VMEM((WIDTH, CHUNK), BF16)
     return pl.pallas_call(
         gram_kernel,
-        grid=(slots // CHUNK,),
-        in_specs=[
-            pl.BlockSpec(memory_space=pltpu.SMEM),
-            pl.BlockSpec((P_COV, CHUNK), lambda i: (0, i)),
-            per_row,
-            per_row,
-            per_row,
-        ],
-        out_specs=pl.BlockSpec((SLAB_ROWS, 128), lambda i: (0, 0)),
+        in_specs=[pl.BlockSpec(memory_space=pltpu.SMEM), in_place, in_place, in_place, in_place],
         out_shape=jax.ShapeDtypeStruct((SLAB_ROWS, 128), F32),
         scratch_shapes=[
-            pltpu.VMEM((WIDTH, CHUNK), BF16),
-            pltpu.VMEM((WIDTH, CHUNK), BF16),
+            pltpu.VMEM((P_COV, slots), F32),
+            pltpu.VMEM((1, slots), jnp.int32),
+            pltpu.VMEM((1, slots), F32),
+            pltpu.VMEM((1, slots), F32),
+            design,
+            design,
+            design,
+            design,
             pltpu.VMEM((WIDTH, WIDTH), F32),
             pltpu.VMEM((WIDTH, WIDTH), F32),
             pltpu.VMEM((16, 128), F32),
+            pltpu.SemaphoreType.DMA((3,)),
+            pltpu.SemaphoreType.DMA((2,)),
         ],
-        compiler_params=pltpu.CompilerParams(
-            dimension_semantics=("arbitrary",), vmem_limit_bytes=40 * 1024 * 1024
-        ),
+        compiler_params=pltpu.CompilerParams(vmem_limit_bytes=62 * 1024 * 1024),
         name="local_sums",
     )(count, covariates, intervals[None, :], offsets[None, :], responses[None, :])
 
@@ -159,12 +188,13 @@
     return pl.pallas_call(
         lambda a, b: sum_repeat_kernel(parts, copies, a, b),
         out_shape=jax.ShapeDtypeStruct((copies * rows, 128), F32),
+        compiler_params=pltpu.CompilerParams(vmem_limit_bytes=4 * 1024 * 1024),
         name="sum_repeat",
     )(received)
 
 
 def lane_spread(tile, lane):
-    return jnp.broadcast_to(tile[:, lane : lane + 1], tile.shape)
+    return jnp.take_along_axis(tile, jnp.full(tile.shape, lane, jnp.int32), axis=1)
 
 
 def row_spread(tile, row):
@@ -210,36 +240,47 @@
 
 
 def factor_kernel(sums_ref, smooth_ref, factor_ref, proj_ref, half_ref, gram_ref, inv_ref):
-    row = lax.broadcasted_iota(jnp.int32, (P_COV, P_COV), 0)
-    column = lax.broadcasted_iota(jnp.int32, (P_COV, P_COV), 1)
+    row, column, left = slab_masks()
     second = np.zeros((N_BASIS - 2, N_BASIS))
     for i in range(N_BASIS - 2):
         second[i, i : i + 3] = (1.0, -2.0, 1.0)
     penalty = second.T @ second
-    smooth = jnp.where(row == column, smooth_ref[...], 0.0)
-    pieces = {}
-
-    def put(pair, value):
-        j, k = pair
-        value = value * (1.0 / TOTAL_LIVE)
-        if penalty[j, k]:
-            value = value + smooth * float(penalty[j, k])
-        pieces[j, k] = pieces[k, j] = value
+    smooth = jnp.where(row == column, jnp.concatenate([smooth_ref[...], smooth_ref[...]], axis=1), 0.0)
+    slabs, place = {}, {}
+
+    def keep(entry, value):
+        w, j_left, j_right = entry
+        scale = jnp.where(left, float(penalty[j_left, 2 * w]), float(penalty[j_right, 2 * w + 1]))
+        slabs[entry] = value * (1.0 / TOTAL_LIVE) + smooth * scale
+        place[j_left, 2 * w] = entry
+        if j_right >= 2 * w + 1:
+            place[j_right, 2 * w + 1] = entry
 
     for i in range(HALF):
-        r0, c0 = slab_place(i)
-        packed = sums_ref[r0 : r0 + P_COV, c0 : c0 + P_COV]
-        turned = packed.T
-        put(PAIRS[i], jnp.where(row <= column, packed, turned))
-        diagonal = jnp.broadcast_to(sums_ref[DIAG_ROW + i : DIAG_ROW + i + 1, 0:P_COV], (P_COV, P_COV))
-        lower = jnp.where(row > column, packed, turned)
-        put(PAIRS[HALF + i], jnp.where(row == column, diagonal, lower))
-    nothing = jnp.zeros((P_COV, P_COV), F32)
+        packed = sums_ref[i * P_COV : (i + 1) * P_COV, :]
+        turned = jnp.concatenate([packed[:, :P_COV].T, packed[:, P_COV:].T], axis=1)
+        keep(ROW_SLABS[i], jnp.where(row <= column, packed, turned))
+        diagonal = jnp.broadcast_to(sums_ref[DIAG_ROW + i : DIAG_ROW + i + 1, :], (P_COV, 128))
+        keep(ROW_SLABS[HALF + i], jnp.where(row == column, diagonal, jnp.where(row > column, packed, turned)))
+    swapped = {}
+
+    def in_half(j, k, half):
+        pair = (max(j, k), min(j, k))
+        if pair not in place:
+            return None
+        entry = place[pair]
+        if pair[1] % 2 == half:
+            return slabs[entry]
+        if entry not in swapped:
+            swapped[entry] = pltpu.roll(slabs[entry], P_COV, 1)
+        return swapped[entry]
+
+    nothing = jnp.zeros((P_COV, 128), F32)
     for j in range(N_BASIS):
         for w in range(4):
-            half_ref[w, pl.ds(j, P_COV, N_BASIS), :] = jnp.concatenate(
-                [pieces.get((j, 2 * w), nothing), pieces.get((j, 2 * w + 1), nothing)], axis=1
-            )
+            first, second = in_half(j, 2 * w, 0), in_half(j, 2 * w + 1, 1)
+            first, second = (nothing if first is None else first), (nothing if second is None else second)
+            half_ref[w, pl.ds(j, P_COV, N_BASIS), :] = first if first is second else jnp.where(left, first, second)
     for w in range(4):
         for i in range(4):
             turned = half_ref[w, 128 * i : 128 * i + 128, :].T
@@ -306,20 +347,25 @@
     )(sums, smoothing[None, :])
 
 
+NEAR = ("zn", "yn", "core", "x")
+FAR = ("zf", "yf")
+
+
+def exchange(rows, axes, parts):
+    return lax.all_to_all(rows.reshape(parts, -1, 128), axes, 0, 0, tiled=True).reshape(-1, 128)
+
+
 def per_device(covariates, intervals, offsets, responses, counts, smoothing):
     sums = local_sums(counts, covariates, intervals, offsets, responses)
-    received = lax.all_to_all(sums.reshape(32, 16, 128), ("z", "x"), 0, 0, tiled=True)
-    spread = sum_repeat(received.reshape(512, 128), 32, 16)
-    received = lax.all_to_all(spread.reshape(16, 16, 128), ("y", "c"), 0, 0, tiled=True)
-    spread = sum_repeat(received.reshape(256, 128), 16, 32)
-    sums = lax.all_to_all(spread.reshape(32, 16, 128), ("z", "x"), 0, 0, tiled=True)
-    factor, projected = factorize(sums.reshape(512, 128), smoothing)
+    shares = sum_repeat(exchange(sums, NEAR, SHARES), SHARES, 16)
+    shares = sum_repeat(exchange(shares, FAR, 16), 16, SHARES)
+    factor, projected = factorize(exchange(shares, NEAR, SHARES), smoothing)
     return factor, projected[0]
 
 
 def solution(mesh):
-    fine = Mesh(mesh.devices.reshape(8, 8, 2, 4), ("z", "y", "c", "x"))
-    spread = ("z", "y", "c", "x")
+    fine = Mesh(mesh.devices.reshape(4, 2, 4, 2, 2, 4), ("zf", "zn", "yf", "yn", "core", "x"))
+    spread = fine.axis_names
     return jax.shard_map(
         per_device,
         mesh=fine,

time: 100 us -> 87.6 us (0.88)
  blocking collectives: 65.8 us -> 59.5 us
  local copies, waits for them, and re-layouts: 3.86 us -> 0.01 us
  Pallas kernels: 28.8 us -> 26.5 us
    all_to_all x3, blocking collectives: 65.8 us -> 59.5 us  [exchange(): lax.all_to_all(rows.reshape(parts, -1, 128), axes, 0, 0, tiled=True)]
    unnamed x10 -> x2, local copies, waits for them, and re-layouts: 3.86 us -> 0.01 us
    pallas_call x2, Pallas kernels: 3.28 us -> 0.08 us  [sum_repeat(): pl.pallas_call(lambda a, b: sum_repeat_kernel(parts, copies, a, b), out_s...]
    pallas_call x1, Pallas kernels: 4.29 us -> 6.86 us  [local_sums(): pl.pallas_call(gram_kernel, in_specs=[pl.BlockSpec(memory_space=pltpu.SME...]
    pallas_call x1, Pallas kernels: 21.2 us -> 19.6 us  [factorize(): pl.pallas_call(factor_kernel, out_shape=(jax.ShapeDtypeStruct((WIDTH, WID...]
where the time goes in v2:
time: 87.6 us; the launch traced here: 87.3 us
  blocking collectives  59.5 us (68%)
  Pallas kernels  26.5 us (30%)
  between operations  1.3 us (1%)
    all_to_all x3, blocking collectives, exchange(): lax.all_to_all(rows.reshape(parts, -1, 128), axes, 0, 0, tiled=True)  59.5 us
    pallas_call x1, Pallas kernels, factorize(): pl.pallas_call(factor_kernel, out_shape=(jax.ShapeDtypeStruct((WIDTH, WID...  19.6 us
    pallas_call x1, Pallas kernels, local_sums(): pl.pallas_call(gram_kernel, in_specs=[pl.BlockSpec(memory_space=pltpu.SME...  6.86 us

profile of v2, /device:TPU:1, one launch (start us, length us, event | category | flops | bytes accessed | tf_op | source)
XLA Modules:
  0.0 87.3 jit_solution(1808244485965671808)
XLA Ops:
  1.3 0.0 copy-start
  1.3 6.9 %local_sums.1 = f32[512,128]{1,0:T(8,128)} custom-call(s32[1]{0:T(128)S(6)} %copy.8.count_ref, f32[64,8192]{1,0:T(8,128)} %cov_hbm.1, s32[1,8192]{1,0:T(1,128)} %bitcast.18, f32[1,8192]{1,0:T(1,128)} %bitcast.19, f32[1,8192]{1,0:T(1,128)} %bitcast.20), custom_call_target="tpu_custom_call" | custom-call | tf_op jit(solution)/shard_map/local_sums/pallas_call | solution.py:153
  8.2 23.0 %all_to_all.15 = f32[32,16,128]{2,1,0:T(8,128)S(1)} all-to-all(f32[32,16,128]{2,1,0:T(8,128)} %bitcast.17), channel_id=1, replica_groups=mesh['zf'=4,'zn'=2,'yf'=4,'yn'=2,'core'=2,'x'=4] {'zn','yn','core','x'}, dimensions={0} | all-to-all | bytes 524288 | tf_op jit(solution)/shard_map/all_to_all | solution.py:355
  31.2 23.1 %all_to_all.16 = f32[16,16,128]{2,1,0:T(8,128)S(1)} all-to-all(f32[16,16,128]{2,1,0:T(8,128)S(1)} %bitcast.14), channel_id=1, replica_groups=mesh['zf'=4,'zn'=2,'yf'=4,'yn'=2,'core'=2,'x'=4] {'zf','yf'}, dimensions={0} | all-to-all | bytes 262144 | tf_op jit(solution)/shard_map/all_to_all | solution.py:355
  54.3 13.4 %all_to_all.17 = f32[32,16,128]{2,1,0:T(8,128)S(1)} all-to-all(f32[32,16,128]{2,1,0:T(8,128)S(1)} %bitcast.13), channel_id=1, replica_groups=mesh['zf'=4,'zn'=2,'yf'=4,'yn'=2,'core'=2,'x'=4] {'zn','yn','core','x'}, dimensions={0} | all-to-all | bytes 524288 | tf_op jit(solution)/shard_map/all_to_all | solution.py:355
  67.7 0.0 copy-done
  67.7 19.6 %factorize.1 = (f32[512,512]{1,0:T(8,128)}, f32[1,512]{1,0:T(1,128)}) custom-call(f32[512,128]{1,0:T(8,128)S(1)} %bitcast.11, f32[1,64]{1,0:T(1,128)S(1)} %bitcast.16), custom_call_target="tpu_custom_call" | custom-call | tf_op jit(solution)/shard_map/factorize/pallas_call | solution.py:334
  (2 shorter events, 0.1 us)
Async XLA Ops:
  1.3 66.4 %copy-start = (f32[64]{0:T(128)S(1)}, f32[64]{0:T(128)}, u32[]{:S(2)}) copy-start(f32[64]{0:T(128)} %param.11) | copy-start | bytes 772

commit v3 on v2

--- a/solution.py
+++ b/solution.py
@@ -201,27 +201,55 @@
     return jnp.broadcast_to(tile[row : row + 1, :], tile.shape)
 
 
+def three_terms(value):
+    high = value.astype(BF16)
+    rest = value - high.astype(F32)
+    middle = rest.astype(BF16)
+    return high, middle, (rest - middle.astype(F32)).astype(BF16)
+
+
+def float_product_tn(left, right):
+    a, b = three_terms(left), three_terms(right)
+    order = [(0, 0), (0, 1), (1, 0), (1, 1), (0, 2), (2, 0)]
+    return lax.dot_general(
+        jnp.concatenate([a[i] for i, _ in order], axis=0),
+        jnp.concatenate([b[i] for _, i in order], axis=0),
+        TN,
+        preferred_element_type=F32,
+    )
+
+
 def factor_tile(work, side):
     blocks = len(work)
     lanes = lax.broadcasted_iota(jnp.int32, (8, 128), 1)
     subs = lax.broadcasted_iota(jnp.int32, (8, 128), 0)
     factor_rows, inverse_rows = [], []
     for k in range(blocks):
-        columns = [lane_spread(work[k], 8 * k + t) for t in range(8)]
+        if k == 0:
+            columns = [lane_spread(work[0], t) for t in range(8)]
+        if k + 1 < blocks:
+            ahead = [lane_spread(work[k + 1], 8 * k + 8 + t) for t in range(8)]
         entry = {(s, t): row_spread(columns[t], s) for t in range(8) for s in range(t, 8)}
         rows = [row_spread(work[k], t) for t in range(8)]
         siderows = [row_spread(side[k], t) for t in range(8)]
-        reciprocals, scale = [], {}
+        pivot = entry[0, 0]
+        pivots, reciprocals, scale = [], [], {}
         for t in range(8):
-            reciprocals.append(1.0 / entry[t, t])
+            reciprocal = 1.0 / pivot
+            pivots.append(pivot)
+            reciprocals.append(reciprocal)
+            if t + 1 < 8:
+                pivot = entry[t + 1, t + 1] - (entry[t + 1, t] * entry[t + 1, t]) * reciprocal
             for s in range(t + 1, 8):
-                scale[s, t] = entry[s, t] * reciprocals[t]
+                scale[s, t] = entry[s, t] * reciprocal
             for s in range(t + 1, 8):
                 for u in range(t + 1, s + 1):
-                    entry[s, u] = entry[s, u] - scale[s, t] * entry[u, t]
+                    if (s, u) != (t + 1, t + 1):
+                        entry[s, u] = entry[s, u] - scale[s, t] * entry[u, t]
                 rows[s] = rows[s] - scale[s, t] * rows[t]
                 siderows[s] = siderows[s] - scale[s, t] * siderows[t]
-        for b in range(k + 1, blocks):
+        near = k + 3 if k % 2 else k + 4
+        for b in range(k + 1, min(near, blocks)):
             c = [lane_spread(work[b], 8 * k + t) for t in range(8)]
             for t in range(8):
                 for s in range(t + 1, 8):
@@ -229,13 +257,24 @@
                 weight = c[t] * reciprocals[t]
                 work[b] = work[b] - weight * rows[t]
                 side[b] = side[b] - weight * siderows[t]
+                if b == k + 1:
+                    ahead = [ahead[u] - weight * row_spread(c[t], u) for u in range(8)]
+        if k + 1 < blocks:
+            columns = ahead
         out, sideout = jnp.zeros((8, 128), F32), jnp.zeros((8, 128), F32)
         for t in range(8):
-            root = lax.rsqrt(entry[t, t])
+            root = lax.rsqrt(pivots[t])
             out = jnp.where(subs == t, rows[t] * root, out)
             sideout = jnp.where(subs == t, siderows[t] * root, sideout)
         factor_rows.append(jnp.where(lanes >= subs + 8 * k, out, 0.0))
         inverse_rows.append(jnp.where(lanes <= subs + 8 * k, sideout, 0.0))
+        if k % 2 and near < blocks:
+            upper = jnp.concatenate(factor_rows[k - 1 :], axis=0)
+            both = jnp.concatenate([upper, jnp.concatenate(inverse_rows[k - 1 :], axis=0)], axis=1)
+            change = float_product_tn(upper, both)
+            for b in range(near, blocks):
+                work[b] = work[b] - change[8 * b : 8 * b + 8, :128]
+                side[b] = side[b] - change[8 * b : 8 * b + 8, 128:]
     return factor_rows, inverse_rows
 
 
@@ -284,8 +323,9 @@
     for w in range(4):
         for i in range(4):
             turned = half_ref[w, 128 * i : 128 * i + 128, :].T
+            above = 16 * (i + 1)
             for k in (2 * w, 2 * w + 1):
-                gram_ref[i, pl.ds(k, P_COV, N_BASIS), :] = turned[(k - 2 * w) * P_COV : (k - 2 * w + 1) * P_COV, :]
+                gram_ref[i, pl.ds(k, above, N_BASIS), :] = turned[(k - 2 * w) * P_COV : (k - 2 * w) * P_COV + above, :]
     moment = sums_ref[MOMENT_ROW : MOMENT_ROW + N_BASIS, 0:P_COV].T * (1.0 / math.sqrt(TOTAL_LIVE))
     for j in range(N_BASIS):
         gram_ref[4, pl.ds(j, P_COV, N_BASIS), :] = jnp.broadcast_to(moment[:, j : j + 1], (P_COV, 128))

time: 87.6 us -> 82.8 us (0.945)
  blocking collectives: 59.5 us -> 55.3 us
    pallas_call x1, Pallas kernels: 19.6 us -> 14.8 us  [factorize(): pl.pallas_call(factor_kernel, out_shape=(jax.ShapeDtypeStruct((WIDTH, WID...]
    pallas_call x1, Pallas kernels: 6.86 us -> 11.1 us  [local_sums(): pl.pallas_call(gram_kernel, in_specs=[pl.BlockSpec(memory_space=pltpu.SME...]
    all_to_all x3, blocking collectives: 59.5 us -> 55.3 us  [exchange(): lax.all_to_all(rows.reshape(parts, -1, 128), axes, 0, 0, tiled=True)]
where the time goes in v3:
time: 82.8 us; the launch traced here: 82.6 us
  blocking collectives  55.3 us (67%)
  Pallas kernels  26 us (31%)
  between operations  1.3 us (2%)
    all_to_all x3, blocking collectives, exchange(): lax.all_to_all(rows.reshape(parts, -1, 128), axes, 0, 0, tiled=True)  55.3 us
    pallas_call x1, Pallas kernels, factorize(): pl.pallas_call(factor_kernel, out_shape=(jax.ShapeDtypeStruct((WIDTH, WID...  14.8 us
    pallas_call x1, Pallas kernels, local_sums(): pl.pallas_call(gram_kernel, in_specs=[pl.BlockSpec(memory_space=pltpu.SME...  11.1 us

profile of v3, /device:TPU:1, one launch (start us, length us, event | category | flops | bytes accessed | tf_op | source)
XLA Modules:
  0.0 82.6 jit_solution(10825604330624699374)
XLA Ops:
  1.3 0.0 copy-start
  1.3 11.1 %local_sums.1 = f32[512,128]{1,0:T(8,128)} custom-call(s32[1]{0:T(128)S(6)} %copy.8.count_ref, f32[64,8192]{1,0:T(8,128)} %cov_hbm.1, s32[1,8192]{1,0:T(1,128)} %bitcast.18, f32[1,8192]{1,0:T(1,128)} %bitcast.19, f32[1,8192]{1,0:T(1,128)} %bitcast.20), custom_call_target="tpu_custom_call" | custom-call | tf_op jit(solution)/shard_map/local_sums/pallas_call | solution.py:153
  12.4 18.8 %all_to_all.15 = f32[32,16,128]{2,1,0:T(8,128)S(1)} all-to-all(f32[32,16,128]{2,1,0:T(8,128)} %bitcast.17), channel_id=1, replica_groups=mesh['zf'=4,'zn'=2,'yf'=4,'yn'=2,'core'=2,'x'=4] {'zn','yn','core','x'}, dimensions={0} | all-to-all | bytes 524288 | tf_op jit(solution)/shard_map/all_to_all | solution.py:395
  31.2 23.1 %all_to_all.16 = f32[16,16,128]{2,1,0:T(8,128)S(1)} all-to-all(f32[16,16,128]{2,1,0:T(8,128)S(1)} %bitcast.14), channel_id=1, replica_groups=mesh['zf'=4,'zn'=2,'yf'=4,'yn'=2,'core'=2,'x'=4] {'zf','yf'}, dimensions={0} | all-to-all | bytes 262144 | tf_op jit(solution)/shard_map/all_to_all | solution.py:395
  54.3 13.4 %all_to_all.17 = f32[32,16,128]{2,1,0:T(8,128)S(1)} all-to-all(f32[32,16,128]{2,1,0:T(8,128)S(1)} %bitcast.13), channel_id=1, replica_groups=mesh['zf'=4,'zn'=2,'yf'=4,'yn'=2,'core'=2,'x'=4] {'zn','yn','core','x'}, dimensions={0} | all-to-all | bytes 524288 | tf_op jit(solution)/shard_map/all_to_all | solution.py:395
  67.7 0.0 copy-done
  67.7 14.8 %factorize.1 = (f32[512,512]{1,0:T(8,128)}, f32[1,512]{1,0:T(1,128)}) custom-call(f32[512,128]{1,0:T(8,128)S(1)} %bitcast.11, f32[1,64]{1,0:T(1,128)S(1)} %bitcast.16), custom_call_target="tpu_custom_call" | custom-call | tf_op jit(solution)/shard_map/factorize/pallas_call | solution.py:374
  (2 shorter events, 0.1 us)
Async XLA Ops:
  1.3 66.5 %copy-start = (f32[64]{0:T(128)S(1)}, f32[64]{0:T(128)}, u32[]{:S(2)}) copy-start(f32[64]{0:T(128)} %param.11) | copy-start | bytes 772

commit v4 on v3

--- a/solution.py
+++ b/solution.py
@@ -11,7 +11,8 @@
 P_COV = 64
 N_BASIS = 8
 WIDTH = P_COV * N_BASIS
-CHUNK = 1024
+CHUNK = 2048
+UNROLL = 2
 TOTAL_LIVE = 2097152
 F32 = jnp.float32
 BF16 = jnp.bfloat16
@@ -29,6 +30,18 @@
 TN = (((0,), (0,)), ((), ()))
 
 
+HI_SUMS = [(0, 7), (0, 6), (1, 7)]
+LO_SUMS = [(0, 7), (0, 5), (1, 6), (2, 7)]
+MID_ROWS = [8, 1, 6, 2, 3, 4, 5]
+MID_PLACE = {0: 0, 7: 0, 1: 1, 6: 2, 2: 3, 3: 4, 4: 5, 5: 6}
+END_HI_ROWS = [9, 10]
+END_LO_ROWS = [9, 10, 11, 3, 4]
+
+
+def basis_rows(j):
+    return slice(j * P_COV, (j + 1) * P_COV)
+
+
 def slab_masks():
     row = lax.broadcasted_iota(jnp.int32, (P_COV, 128), 0)
     column = lax.broadcasted_iota(jnp.int32, (P_COV, 128), 1)
@@ -37,7 +50,7 @@
 
 def gram_kernel(
     count_ref, cov_hbm, int_hbm, off_hbm, resp_hbm, out_ref,
-    cov_ref, int_ref, off_ref, resp_ref, hi_even, hi_odd, lo_even, lo_odd, hh_ref, lh_ref, mom_ref, row_sem, cov_sem,
+    cov_ref, int_ref, off_ref, resp_ref, hi_even, hi_odd, lo_even, lo_odd, mid_ref, end_ref, mom_ref, row_sem, cov_sem,
 ):
     count = count_ref[0]
     chunks = cov_hbm.shape[1] // CHUNK
@@ -49,20 +62,24 @@
         pltpu.make_async_copy(source, target, row_sem.at[i])
         for i, (source, target) in enumerate([(int_hbm, int_ref), (off_hbm, off_ref), (resp_hbm, resp_ref)])
     ]
-    cov_copies = [
-        pltpu.make_async_copy(cov_hbm.at[:, part], cov_ref.at[:, part], cov_sem.at[i])
-        for i, part in enumerate([slice(0, CHUNK), slice(CHUNK, chunks * CHUNK)])
-    ]
-    for copy in [*row_copies, *cov_copies]:
+    groups = chunks // UNROLL
+
+    def cov_copy(i):
+        part = pl.ds(pl.multiple_of(i * UNROLL * CHUNK, UNROLL * CHUNK), UNROLL * CHUNK)
+        return pltpu.make_async_copy(cov_hbm.at[:, part], cov_ref.at[:, part], cov_sem.at[i])
+
+    for copy in row_copies:
         copy.start()
-    hh_ref[...] = jnp.zeros_like(hh_ref)
-    lh_ref[...] = jnp.zeros_like(lh_ref)
+    for i in range(groups):
+        cov_copy(i).start()
+    mid_ref[...] = jnp.zeros_like(mid_ref)
+    end_ref[...] = jnp.zeros_like(end_ref)
     mom_ref[...] = jnp.zeros_like(mom_ref)
     for copy in row_copies:
         copy.wait()
 
     def build(c, hi_ref, lo_ref):
-        part = columns(jnp.minimum(c, chunks - 1))
+        part = columns(c)
         cov = cov_ref[:, part]
         interval = int_ref[:, part]
         within = off_ref[:, part]
@@ -75,7 +92,7 @@
         second = (3.0 * cube - 6.0 * square + 4.0) * (1.0 / 6.0) * live
         third = (-3.0 * cube + 3.0 * square + 3.0 * within + 1.0) * (1.0 / 6.0) * live
         fourth = cube * (1.0 / 6.0) * live
-        weights = []
+        weights, highs, lows = [], [], []
         for j in range(N_BASIS):
             value = jnp.where(interval == j, first, 0.0)
             value = jnp.where(interval + 1 == j, second, value)
@@ -83,9 +100,14 @@
             value = jnp.where(interval + 3 == j, fourth, value)
             weights.append(value)
             design = cov * value
-            high = design.astype(BF16)
-            hi_ref[j * P_COV : (j + 1) * P_COV, :] = high
-            lo_ref[j * P_COV : (j + 1) * P_COV, :] = (design - high.astype(F32)).astype(BF16)
+            highs.append(design.astype(BF16))
+            lows.append((design - highs[j].astype(F32)).astype(BF16))
+            hi_ref[basis_rows(j), :] = highs[j]
+            lo_ref[basis_rows(j), :] = lows[j]
+        for i, (j, k) in enumerate(HI_SUMS):
+            hi_ref[basis_rows(N_BASIS + i), :] = highs[j] + highs[k]
+        for i, (j, k) in enumerate(LO_SUMS):
+            lo_ref[basis_rows(N_BASIS + i), :] = lows[j] + lows[k]
         cov_high = cov.astype(BF16)
         cov_low = (cov - cov_high.astype(F32)).astype(BF16)
         weighted = jnp.concatenate(weights, axis=0) * resp_ref[:, part]
@@ -99,30 +121,50 @@
         )
 
     def multiply(hi_ref, lo_ref):
-        def product(left_ref, rows, columns):
-            return lax.dot_general(left_ref[rows, :], hi_ref[columns, :], NT, preferred_element_type=F32)
-
-        low, high_half = slice(0, 256), slice(256, 512)
-        hh_ref[0:448, low] += product(hi_ref, slice(0, 448), low)
-        lh_ref[0:448, low] += product(lo_ref, slice(0, 448), low)
-        hh_ref[high_half, high_half] += product(hi_ref, high_half, high_half)
-        lh_ref[64:512, high_half] += product(lo_ref, slice(64, 512), high_half)
-
-    cov_copies[0].wait()
-    build(0, hi_even, lo_even)
-    cov_copies[1].wait()
-
-    def pair(i, _):
-        build(2 * i + 1, hi_odd, lo_odd)
-        multiply(hi_even, lo_even)
-        build(2 * i + 2, hi_even, lo_even)
-        multiply(hi_odd, lo_odd)
+        def rows_of(ref, places):
+            return [ref[basis_rows(place), :] for place in places]
+
+        middle = jnp.concatenate(rows_of(hi_ref, MID_ROWS) + rows_of(lo_ref, MID_ROWS), axis=0)
+        mid_ref[...] += lax.dot_general(middle, hi_ref[128:384, :], NT, preferred_element_type=F32)
+        ends = jnp.concatenate(rows_of(hi_ref, END_HI_ROWS) + rows_of(lo_ref, END_LO_ROWS), axis=0)
+        across = jnp.concatenate([hi_ref[0:128, :], hi_ref[384:512, :]], axis=0)
+        end_ref[...] += lax.dot_general(ends, across, NT, preferred_element_type=F32)
+
+    def group(i, _):
+        cov_copy(i).wait()
+        for c in range(UNROLL):
+            hi_ref, lo_ref = (hi_odd, lo_odd) if c % 2 else (hi_even, lo_even)
+            build(UNROLL * i + c, hi_ref, lo_ref)
+            multiply(hi_ref, lo_ref)
         return 0
 
-    lax.fori_loop(0, pl.cdiv(count, 2 * CHUNK), pair, 0)
+    def unused(i, _):
+        cov_copy(i).wait()
+        return 0
+
+    used = pl.cdiv(count, UNROLL * CHUNK)
+    lax.fori_loop(0, used, group, 0)
+    lax.fori_loop(used, groups, unused, 0)
 
     row, column, left = slab_masks()
     tiles = {}
+
+    def high_rows(j, w):
+        if w in (1, 2):
+            return mid_ref[basis_rows(MID_PLACE[j]), 128 * w - 128 : 128 * w]
+        return end_ref[basis_rows(j % 6), 0:128] if w == 0 else end_ref[basis_rows(j - 6), 128:256]
+
+    def low_rows(j, w):
+        if w in (1, 2):
+            return mid_ref[basis_rows(len(MID_ROWS) + MID_PLACE[j]), 128 * w - 128 : 128 * w]
+        place = len(END_HI_ROWS) + (j if j < 5 else j - 5)
+        return end_ref[basis_rows(place), 0:128] if w == 0 else end_ref[basis_rows(place), 128:256]
+
+    def tile(t, w):
+        turn_high = w == 0 and t in (1, 2)
+        straight = [low_rows(j, w) if turn_high else low_rows(j, w) + high_rows(j, w) for j in (2 * t, 2 * t + 1)]
+        turned = [low_rows(k, t) + high_rows(k, t) if turn_high else low_rows(k, t) for k in (2 * w, 2 * w + 1)]
+        return jnp.concatenate(straight, axis=0) + jnp.concatenate(turned, axis=0).T
 
     def row_slab(entry):
         w, j_left, j_right = entry
@@ -130,8 +172,7 @@
         for j in (j_left, j_right):
             t = j // 2
             if (t, w) not in tiles:
-                at, across = slice(128 * t, 128 * t + 128), slice(128 * w, 128 * w + 128)
-                tiles[t, w] = hh_ref[at, across] + lh_ref[at, across] + lh_ref[across, at].T
+                tiles[t, w] = tile(t, w)
             pieces.append(tiles[t, w][(j % 2) * P_COV : (j % 2 + 1) * P_COV, :])
         return pieces[0] if j_left == j_right else jnp.where(left, pieces[0], pieces[1])
 
@@ -149,7 +190,8 @@
 def local_sums(count, covariates, intervals, offsets, responses):
     slots = covariates.shape[1]
     in_place = pl.BlockSpec(memory_space=pltpu.HBM)
-    design = pltpu.VMEM((WIDTH, CHUNK), BF16)
+    high = pltpu.VMEM((WIDTH + len(HI_SUMS) * P_COV, CHUNK), BF16)
+    low = pltpu.VMEM((WIDTH + len(LO_SUMS) * P_COV, CHUNK), BF16)
     return pl.pallas_call(
         gram_kernel,
         in_specs=[pl.BlockSpec(memory_space=pltpu.SMEM), in_place, in_place, in_place, in_place],
@@ -159,15 +201,15 @@
             pltpu.VMEM((1, slots), jnp.int32),
             pltpu.VMEM((1, slots), F32),
             pltpu.VMEM((1, slots), F32),
-            design,
-            design,
-            design,
-            design,
-            pltpu.VMEM((WIDTH, WIDTH), F32),
-            pltpu.VMEM((WIDTH, WIDTH), F32),
+            high,
+            high,
+            low,
+            low,
+            pltpu.VMEM((2 * len(MID_ROWS) * P_COV, 256), F32),
+            pltpu.VMEM(((len(END_HI_ROWS) + len(END_LO_ROWS)) * P_COV, 256), F32),
             pltpu.VMEM((16, 128), F32),
             pltpu.SemaphoreType.DMA((3,)),
-            pltpu.SemaphoreType.DMA((2,)),
+            pltpu.SemaphoreType.DMA((slots // (UNROLL * CHUNK),)),
         ],
         compiler_params=pltpu.CompilerParams(vmem_limit_bytes=62 * 1024 * 1024),
         name="local_sums",
@@ -208,13 +250,15 @@
     return high, middle, (rest - middle.astype(F32)).astype(BF16)
 
 
-def float_product_tn(left, right):
-    a, b = three_terms(left), three_terms(right)
-    order = [(0, 0), (0, 1), (1, 0), (1, 1), (0, 2), (2, 0)]
+TERM_PAIRS = [(0, 0), (0, 1), (1, 0), (1, 1), (0, 2), (2, 0)]
+
+
+def float_product(left_terms, right_terms, contract):
+    left_axis, right_axis = contract
     return lax.dot_general(
-        jnp.concatenate([a[i] for i, _ in order], axis=0),
-        jnp.concatenate([b[i] for _, i in order], axis=0),
-        TN,
+        jnp.concatenate([left_terms[i] for i, _ in TERM_PAIRS], axis=left_axis),
+        jnp.concatenate([right_terms[i] for _, i in TERM_PAIRS], axis=right_axis),
+        (((left_axis,), (right_axis,)), ((), ())),
         preferred_element_type=F32,
     )
 
@@ -271,7 +315,7 @@
         if k % 2 and near < blocks:
             upper = jnp.concatenate(factor_rows[k - 1 :], axis=0)
             both = jnp.concatenate([upper, jnp.concatenate(inverse_rows[k - 1 :], axis=0)], axis=1)
-            change = float_product_tn(upper, both)
+            change = float_product(three_terms(upper), three_terms(both), (0, 0))
             for b in range(near, blocks):
                 work[b] = work[b] - change[8 * b : 8 * b + 8, :128]
                 side[b] = side[b] - change[8 * b : 8 * b + 8, 128:]
@@ -348,18 +392,22 @@
             @pl.when(p == q)
             def _():
                 mine = slice(128 * q, 128 * q + 128)
-                inverse = inv_ref[...]
-                solved = {}
+                right = jnp.concatenate([gram_ref[w, mine, :] for w in range(q + 1, 5)], axis=1)
+                solved = float_product(three_terms(inv_ref[...]), three_terms(right), (1, 0))
+                terms = three_terms(solved)
                 for w in range(q + 1, 5):
-                    solved[w] = jnp.dot(inverse, gram_ref[w, mine, :], precision=HIGHEST, preferred_element_type=F32)
-                    gram_ref[w, mine, :] = solved[w]
+                    part = solved[:, 128 * (w - q - 1) : 128 * (w - q)]
                     if w < 4:
-                        factor_ref[mine, 128 * w : 128 * w + 128] = solved[w]
+                        factor_ref[mine, 128 * w : 128 * w + 128] = part
+                    else:
+                        gram_ref[w, mine, :] = part
                 for i in range(q + 1, 4):
+                    at = 128 * (i - q - 1)
+                    change = float_product(
+                        [term[:, at : at + 128] for term in terms], [term[:, at:] for term in terms], (0, 0)
+                    )
                     for w in range(i, 5):
-                        gram_ref[w, 128 * i : 128 * i + 128, :] -= lax.dot_general(
-                            solved[i], solved[w], TN, precision=HIGHEST, preferred_element_type=F32
-                        )
+                        gram_ref[w, 128 * i : 128 * i + 128, :] -= change[:, 128 * (w - i) : 128 * (w - i) + 128]
 
         return 0
 

time: 82.8 us -> 80.2 us (0.969)
  Pallas kernels: 26 us -> 23.5 us
    pallas_call x1, Pallas kernels: 11.1 us -> 9 us  [local_sums(): pl.pallas_call(gram_kernel, in_specs=[pl.BlockSpec(memory_space=pltpu.SME...]
where the time goes in v4:
time: 80.2 us; the launch traced here: 79.9 us
  blocking collectives  55.1 us (69%)
  Pallas kernels  23.5 us (29%)
  between operations  1.3 us (2%)
    all_to_all x3, blocking collectives, exchange(): lax.all_to_all(rows.reshape(parts, -1, 128), axes, 0, 0, tiled=True)  55.1 us
    pallas_call x1, Pallas kernels, factorize(): pl.pallas_call(factor_kernel, out_shape=(jax.ShapeDtypeStruct((WIDTH, WID...  14.4 us
    pallas_call x1, Pallas kernels, local_sums(): pl.pallas_call(gram_kernel, in_specs=[pl.BlockSpec(memory_space=pltpu.SME...  9 us

profile of v4, /device:TPU:1, one launch (start us, length us, event | category | flops | bytes accessed | tf_op | source)
XLA Modules:
  0.0 79.9 jit_solution(1811117680070541071)
XLA Ops:
  1.3 0.0 copy-start
  1.3 9.0 %local_sums.1 = f32[512,128]{1,0:T(8,128)} custom-call(s32[1]{0:T(128)S(6)} %copy.8.count_ref, f32[64,8192]{1,0:T(8,128)} %cov_hbm.1, s32[1,8192]{1,0:T(1,128)} %bitcast.18, f32[1,8192]{1,0:T(1,128)} %bitcast.19, f32[1,8192]{1,0:T(1,128)} %bitcast.20), custom_call_target="tpu_custom_call" | custom-call | tf_op jit(solution)/shard_map/local_sums/pallas_call | solution.py:195
  10.3 16.8 %all_to_all.15 = f32[32,16,128]{2,1,0:T(8,128)S(1)} all-to-all(f32[32,16,128]{2,1,0:T(8,128)} %bitcast.17), channel_id=1, replica_groups=mesh['zf'=4,'zn'=2,'yf'=4,'yn'=2,'core'=2,'x'=4] {'zn','yn','core','x'}, dimensions={0} | all-to-all | bytes 524288 | tf_op jit(solution)/shard_map/all_to_all | solution.py:443
  27.1 24.9 %all_to_all.16 = f32[16,16,128]{2,1,0:T(8,128)S(1)} all-to-all(f32[16,16,128]{2,1,0:T(8,128)S(1)} %bitcast.14), channel_id=1, replica_groups=mesh['zf'=4,'zn'=2,'yf'=4,'yn'=2,'core'=2,'x'=4] {'zf','yf'}, dimensions={0} | all-to-all | bytes 262144 | tf_op jit(solution)/shard_map/all_to_all | solution.py:443
  52.1 13.4 %all_to_all.17 = f32[32,16,128]{2,1,0:T(8,128)S(1)} all-to-all(f32[32,16,128]{2,1,0:T(8,128)S(1)} %bitcast.13), channel_id=1, replica_groups=mesh['zf'=4,'zn'=2,'yf'=4,'yn'=2,'core'=2,'x'=4] {'zn','yn','core','x'}, dimensions={0} | all-to-all | bytes 524288 | tf_op jit(solution)/shard_map/all_to_all | solution.py:443
  65.5 0.0 copy-done
  65.5 14.4 %factorize.1 = (f32[512,512]{1,0:T(8,128)}, f32[1,512]{1,0:T(1,128)}) custom-call(f32[512,128]{1,0:T(8,128)S(1)} %bitcast.11, f32[1,64]{1,0:T(1,128)S(1)} %bitcast.16), custom_call_target="tpu_custom_call" | custom-call | tf_op jit(solution)/shard_map/factorize/pallas_call | solution.py:422
  (2 shorter events, 0.1 us)
Async XLA Ops:
  1.3 64.2 %copy-start = (f32[64]{0:T(128)S(1)}, f32[64]{0:T(128)}, u32[]{:S(2)}) copy-start(f32[64]{0:T(128)} %param.11) | copy-start | bytes 772

commit v5 on v4

--- a/solution.py
+++ b/solution.py
@@ -263,11 +263,11 @@
     )
 
 
-def factor_tile(work, side):
+def factor_tile(work, side, side_is_identity):
     blocks = len(work)
     lanes = lax.broadcasted_iota(jnp.int32, (8, 128), 1)
     subs = lax.broadcasted_iota(jnp.int32, (8, 128), 0)
-    factor_rows, inverse_rows = [], []
+    factor_rows, solved_rows = [], []
     for k in range(blocks):
         if k == 0:
             columns = [lane_spread(work[0], t) for t in range(8)]
@@ -311,52 +311,61 @@
             out = jnp.where(subs == t, rows[t] * root, out)
             sideout = jnp.where(subs == t, siderows[t] * root, sideout)
         factor_rows.append(jnp.where(lanes >= subs + 8 * k, out, 0.0))
-        inverse_rows.append(jnp.where(lanes <= subs + 8 * k, sideout, 0.0))
+        solved_rows.append(jnp.where(lanes <= subs + 8 * k, sideout, 0.0) if side_is_identity else sideout)
         if k % 2 and near < blocks:
             upper = jnp.concatenate(factor_rows[k - 1 :], axis=0)
-            both = jnp.concatenate([upper, jnp.concatenate(inverse_rows[k - 1 :], axis=0)], axis=1)
+            both = jnp.concatenate([upper, jnp.concatenate(solved_rows[k - 1 :], axis=0)], axis=1)
             change = float_product(three_terms(upper), three_terms(both), (0, 0))
             for b in range(near, blocks):
                 work[b] = work[b] - change[8 * b : 8 * b + 8, :128]
                 side[b] = side[b] - change[8 * b : 8 * b + 8, 128:]
-    return factor_rows, inverse_rows
-
-
-def factor_kernel(sums_ref, smooth_ref, factor_ref, proj_ref, half_ref, gram_ref, inv_ref):
+    return factor_rows, solved_rows
+
+
+def factor_kernel(sums_ref, smooth_ref, factor_ref, proj_ref, half_ref, gram_ref):
     row, column, left = slab_masks()
     second = np.zeros((N_BASIS - 2, N_BASIS))
     for i in range(N_BASIS - 2):
         second[i, i : i + 3] = (1.0, -2.0, 1.0)
     penalty = second.T @ second
     smooth = jnp.where(row == column, jnp.concatenate([smooth_ref[...], smooth_ref[...]], axis=1), 0.0)
-    slabs, place = {}, {}
-
-    def keep(entry, value):
-        w, j_left, j_right = entry
-        scale = jnp.where(left, float(penalty[j_left, 2 * w]), float(penalty[j_right, 2 * w + 1]))
-        slabs[entry] = value * (1.0 / TOTAL_LIVE) + smooth * scale
-        place[j_left, 2 * w] = entry
+    diagonals = sums_ref[DIAG_ROW : DIAG_ROW + 8, :]
+    diagonals = (diagonals, pltpu.roll(diagonals, P_COV, 1))
+    packed, turned = {}, {}
+    for i in range(0, HALF, 2):
+        both = sums_ref[i * P_COV : (i + 2) * P_COV, :]
+        top, bottom = both.T[:P_COV], both.T[P_COV:]
+        top_moved, bottom_moved = pltpu.roll(top, P_COV, 1), pltpu.roll(bottom, P_COV, 1)
+        packed[i], packed[i + 1] = both[:P_COV], both[P_COV:]
+        turned[i, 0] = jnp.where(left, top, bottom_moved)
+        turned[i, 1] = jnp.where(left, bottom, top_moved)
+        turned[i + 1, 0] = jnp.where(left, top_moved, bottom)
+        turned[i + 1, 1] = jnp.where(left, bottom_moved, top)
+    place, slabs = {}, {}
+    for number, (w, j_left, j_right) in enumerate(ROW_SLABS):
+        place[j_left, 2 * w] = number
         if j_right >= 2 * w + 1:
-            place[j_right, 2 * w + 1] = entry
-
-    for i in range(HALF):
-        packed = sums_ref[i * P_COV : (i + 1) * P_COV, :]
-        turned = jnp.concatenate([packed[:, :P_COV].T, packed[:, P_COV:].T], axis=1)
-        keep(ROW_SLABS[i], jnp.where(row <= column, packed, turned))
-        diagonal = jnp.broadcast_to(sums_ref[DIAG_ROW + i : DIAG_ROW + i + 1, :], (P_COV, 128))
-        keep(ROW_SLABS[HALF + i], jnp.where(row == column, diagonal, jnp.where(row > column, packed, turned)))
-    swapped = {}
+            place[j_right, 2 * w + 1] = number
+
+    def slab(number, swap):
+        if (number, swap) not in slabs:
+            i = number % HALF
+            straight = pltpu.roll(packed[i], P_COV, 1) if swap else packed[i]
+            if number < HALF:
+                value = jnp.where(row <= column, straight, turned[i, swap])
+            else:
+                diagonal = jnp.broadcast_to(diagonals[swap][i : i + 1, :], (P_COV, 128))
+                value = jnp.where(row > column, straight, turned[i, swap])
+                value = jnp.where(row == column, diagonal, value)
+            w, j_left, j_right = ROW_SLABS[number]
+            factors = (float(penalty[j_left, 2 * w]), float(penalty[j_right, 2 * w + 1]))
+            scale = jnp.where(left, factors[swap], factors[1 - swap])
+            slabs[number, swap] = value * (1.0 / TOTAL_LIVE) + smooth * scale
+        return slabs[number, swap]
 
     def in_half(j, k, half):
         pair = (max(j, k), min(j, k))
-        if pair not in place:
-            return None
-        entry = place[pair]
-        if pair[1] % 2 == half:
-            return slabs[entry]
-        if entry not in swapped:
-            swapped[entry] = pltpu.roll(slabs[entry], P_COV, 1)
-        return swapped[entry]
+        return slab(place[pair], int(pair[1] % 2 != half)) if pair in place else None
 
     nothing = jnp.zeros((P_COV, 128), F32)
     for j in range(N_BASIS):
@@ -378,40 +387,34 @@
     lanes = lax.broadcasted_iota(jnp.int32, (8, 128), 1)
     subs = lax.broadcasted_iota(jnp.int32, (8, 128), 0)
 
-    def panel(p, _):
-        start = pl.multiple_of(p * 128, 128)
-        work = [gram_ref[p, pl.ds(pl.multiple_of(start + 8 * b, 8), 8), :] for b in range(16)]
-        side = [jnp.where(lanes == subs + 8 * b, 1.0, 0.0).astype(F32) for b in range(16)]
-        factor_rows, inverse_rows = factor_tile(work, side)
-        for b in range(16):
-            inv_ref[8 * b : 8 * b + 8, :] = inverse_rows[b]
-            factor_ref[pl.ds(pl.multiple_of(start + 8 * b, 8), 8), pl.ds(start, 128)] = factor_rows[b]
-
-        for q in range(4):
-
-            @pl.when(p == q)
-            def _():
-                mine = slice(128 * q, 128 * q + 128)
-                right = jnp.concatenate([gram_ref[w, mine, :] for w in range(q + 1, 5)], axis=1)
-                solved = float_product(three_terms(inv_ref[...]), three_terms(right), (1, 0))
-                terms = three_terms(solved)
-                for w in range(q + 1, 5):
-                    part = solved[:, 128 * (w - q - 1) : 128 * (w - q)]
-                    if w < 4:
-                        factor_ref[mine, 128 * w : 128 * w + 128] = part
-                    else:
-                        gram_ref[w, mine, :] = part
-                for i in range(q + 1, 4):
-                    at = 128 * (i - q - 1)
-                    change = float_product(
-                        [term[:, at : at + 128] for term in terms], [term[:, at:] for term in terms], (0, 0)
-                    )
-                    for w in range(i, 5):
-                        gram_ref[w, 128 * i : 128 * i + 128, :] -= change[:, 128 * (w - i) : 128 * (w - i) + 128]
-
-        return 0
-
-    lax.fori_loop(0, 4, panel, 0)
+    for p in range(4):
+        mine = slice(128 * p, 128 * p + 128)
+        work = [gram_ref[p, 128 * p + 8 * b : 128 * p + 8 * b + 8, :] for b in range(16)]
+        last = p == 3
+        if last:
+            side = [gram_ref[4, 128 * p + 8 * b : 128 * p + 8 * b + 8, :] for b in range(16)]
+        else:
+            side = [jnp.where(lanes == subs + 8 * b, 1.0, 0.0).astype(F32) for b in range(16)]
+        factor_rows, solved_rows = factor_tile(work, side, not last)
+        factor_ref[mine, mine] = jnp.concatenate(factor_rows, axis=0)
+        if last:
+            gram_ref[4, mine, :] = jnp.concatenate(solved_rows, axis=0)
+            break
+        inverse = jnp.concatenate(solved_rows, axis=0)
+        right = jnp.concatenate([gram_ref[w, mine, :] for w in range(p + 1, 5)], axis=1)
+        solved = float_product(three_terms(inverse), three_terms(right), (1, 0))
+        terms = three_terms(solved)
+        for w in range(p + 1, 5):
+            part = solved[:, 128 * (w - p - 1) : 128 * (w - p)]
+            if w < 4:
+                factor_ref[mine, 128 * w : 128 * w + 128] = part
+            else:
+                gram_ref[w, mine, :] = part
+        for i in range(p + 1, 4):
+            at = 128 * (i - p - 1)
+            change = float_product([term[:, at : at + 128] for term in terms], [term[:, at:] for term in terms], (0, 0))
+            for w in range(i, 5):
+                gram_ref[w, 128 * i : 128 * i + 128, :] -= change[:, 128 * (w - i) : 128 * (w - i) + 128]
     diagonal_mask = lax.broadcasted_iota(jnp.int32, (128, 128), 0) == lax.broadcasted_iota(jnp.int32, (128, 128), 1)
     for p in range(4):
         tile = gram_ref[4, 128 * p : 128 * p + 128, :]
@@ -428,7 +431,6 @@
         scratch_shapes=[
             pltpu.VMEM((4, WIDTH, 128), F32),
             pltpu.VMEM((5, WIDTH, 128), F32),
-            pltpu.VMEM((128, 128), F32),
         ],
         compiler_params=pltpu.CompilerParams(vmem_limit_bytes=40 * 1024 * 1024),
         name="factorize",

time: 80.2 us -> 78.9 us (0.984)
  Pallas kernels: 23.5 us -> 18.7 us
  blocking collectives: 55.1 us -> 58.6 us
    all_to_all x3, blocking collectives: 55.1 us -> 58.6 us  [exchange(): lax.all_to_all(rows.reshape(parts, -1, 128), axes, 0, 0, tiled=True)]
    pallas_call x1, Pallas kernels: 9 us -> 5.63 us  [local_sums(): pl.pallas_call(gram_kernel, in_specs=[pl.BlockSpec(memory_space=pltpu.SME...]
    pallas_call x1, Pallas kernels: 14.4 us -> 13 us  [factorize(): pl.pallas_call(factor_kernel, out_shape=(jax.ShapeDtypeStruct((WIDTH, WID...]
where the time goes in v5:
time: 78.9 us; the launch traced here: 78.7 us
  blocking collectives  58.6 us (74%)
  Pallas kernels  18.7 us (24%)
  between operations  1.3 us (2%)
    all_to_all x3, blocking collectives, exchange(): lax.all_to_all(rows.reshape(parts, -1, 128), axes, 0, 0, tiled=True)  58.6 us
    pallas_call x1, Pallas kernels, factorize(): pl.pallas_call(factor_kernel, out_shape=(jax.ShapeDtypeStruct((WIDTH, WID...  13 us
    pallas_call x1, Pallas kernels, local_sums(): pl.pallas_call(gram_kernel, in_specs=[pl.BlockSpec(memory_space=pltpu.SME...  5.63 us

profile of v5, /device:TPU:1, one launch (start us, length us, event | category | flops | bytes accessed | tf_op | source)
XLA Modules:
  0.0 78.7 jit_solution(10082844995289526783)
XLA Ops:
  1.3 0.0 copy-start
  1.3 5.6 %local_sums.1 = f32[512,128]{1,0:T(8,128)} custom-call(s32[1]{0:T(128)S(6)} %copy.8.count_ref, f32[64,8192]{1,0:T(8,128)} %cov_hbm.1, s32[1,8192]{1,0:T(1,128)} %bitcast.18, f32[1,8192]{1,0:T(1,128)} %bitcast.19, f32[1,8192]{1,0:T(1,128)} %bitcast.20), custom_call_target="tpu_custom_call" | custom-call | tf_op jit(solution)/shard_map/local_sums/pallas_call | solution.py:195
  6.9 20.4 %all_to_all.15 = f32[32,16,128]{2,1,0:T(8,128)S(1)} all-to-all(f32[32,16,128]{2,1,0:T(8,128)} %bitcast.17), channel_id=1, replica_groups=mesh['zf'=4,'zn'=2,'yf'=4,'yn'=2,'core'=2,'x'=4] {'zn','yn','core','x'}, dimensions={0} | all-to-all | bytes 524288 | tf_op jit(solution)/shard_map/all_to_all | solution.py:445
  27.4 24.8 %all_to_all.16 = f32[16,16,128]{2,1,0:T(8,128)S(1)} all-to-all(f32[16,16,128]{2,1,0:T(8,128)S(1)} %bitcast.14), channel_id=1, replica_groups=mesh['zf'=4,'zn'=2,'yf'=4,'yn'=2,'core'=2,'x'=4] {'zf','yf'}, dimensions={0} | all-to-all | bytes 262144 | tf_op jit(solution)/shard_map/all_to_all | solution.py:445
  52.2 13.4 %all_to_all.17 = f32[32,16,128]{2,1,0:T(8,128)S(1)} all-to-all(f32[32,16,128]{2,1,0:T(8,128)S(1)} %bitcast.13), channel_id=1, replica_groups=mesh['zf'=4,'zn'=2,'yf'=4,'yn'=2,'core'=2,'x'=4] {'zn','yn','core','x'}, dimensions={0} | all-to-all | bytes 524288 | tf_op jit(solution)/shard_map/all_to_all | solution.py:445
  65.7 0.0 copy-done
  65.7 13.0 %factorize.1 = (f32[512,512]{1,0:T(8,128)}, f32[1,512]{1,0:T(1,128)}) custom-call(f32[512,128]{1,0:T(8,128)S(1)} %bitcast.11, f32[1,64]{1,0:T(1,128)S(1)} %bitcast.16), custom_call_target="tpu_custom_call" | custom-call | tf_op jit(solution)/shard_map/factorize/pallas_call | solution.py:425
  (2 shorter events, 0.1 us)
Async XLA Ops:
  1.3 64.4 %copy-start = (f32[64]{0:T(128)S(1)}, f32[64]{0:T(128)}, u32[]{:S(2)}) copy-start(f32[64]{0:T(128)} %param.11) | copy-start | bytes 772

commit v6 on v5

--- a/solution.py
+++ b/solution.py
@@ -24,8 +24,6 @@
 SHARES = 32
 SHARE_ROWS = 16
 SLAB_ROWS = SHARES * SHARE_ROWS
-DIAG_ROW = HALF * P_COV
-MOMENT_ROW = DIAG_ROW + 8
 NT = (((1,), (1,)), ((), ()))
 TN = (((0,), (0,)), ((), ()))
 
@@ -40,6 +38,15 @@
 
 def basis_rows(j):
     return slice(j * P_COV, (j + 1) * P_COV)
+
+
+def turn(far):
+    return 1 - ((far + 1) // 2) % 2
+
+
+def block_rows(i):
+    exchanged = 4 * turn(lax.axis_index("zf")) + 2 * turn(lax.axis_index("yf"))
+    return pl.ds(pl.multiple_of(jnp.bitwise_xor(jnp.int32(i), exchanged) * P_COV, P_COV), P_COV)
 
 
 def slab_masks():
@@ -176,15 +183,15 @@
             pieces.append(tiles[t, w][(j % 2) * P_COV : (j % 2 + 1) * P_COV, :])
         return pieces[0] if j_left == j_right else jnp.where(left, pieces[0], pieces[1])
 
-    out_ref[DIAG_ROW:, :] = jnp.zeros((SLAB_ROWS - DIAG_ROW, 128), F32)
+    small = [jnp.zeros((P_COV, 128), F32)]
     for i in range(HALF):
         upper, lower = row_slab(ROW_SLABS[i]), row_slab(ROW_SLABS[HALF + i])
-        out_ref[i * P_COV : (i + 1) * P_COV, :] = jnp.where(row <= column, upper, lower)
-        out_ref[DIAG_ROW + i : DIAG_ROW + i + 1, :] = jnp.sum(
-            jnp.where(row == column, lower, 0.0), axis=0, keepdims=True
-        )
+        out_ref[block_rows(i), :] = jnp.where(row <= column, upper, lower)
+        diagonal = jnp.sum(jnp.where(row == column, lower, 0.0), axis=0, keepdims=True)
+        small.append(jnp.where(row == i, diagonal, small[-1]))
     mom = mom_ref[...]
-    out_ref[MOMENT_ROW : MOMENT_ROW + N_BASIS, 0:P_COV] = mom[0:8, 0:P_COV] + mom[8:16, 0:P_COV] + mom[0:8, P_COV:]
+    moment = mom[0:8, :] + mom[8:16, :] + pltpu.roll(mom[0:8, :], P_COV, 1)
+    out_ref[block_rows(HALF), :] = jnp.concatenate([small[-1][0:8], moment, small[-1][16:]], axis=0)
 
 
 def local_sums(count, covariates, intervals, offsets, responses):
@@ -329,11 +336,12 @@
         second[i, i : i + 3] = (1.0, -2.0, 1.0)
     penalty = second.T @ second
     smooth = jnp.where(row == column, jnp.concatenate([smooth_ref[...], smooth_ref[...]], axis=1), 0.0)
-    diagonals = sums_ref[DIAG_ROW : DIAG_ROW + 8, :]
+    small = sums_ref[block_rows(HALF), :]
+    diagonals = small[0:8]
     diagonals = (diagonals, pltpu.roll(diagonals, P_COV, 1))
     packed, turned = {}, {}
     for i in range(0, HALF, 2):
-        both = sums_ref[i * P_COV : (i + 2) * P_COV, :]
+        both = jnp.concatenate([sums_ref[block_rows(i), :], sums_ref[block_rows(i + 1), :]], axis=0)
         top, bottom = both.T[:P_COV], both.T[P_COV:]
         top_moved, bottom_moved = pltpu.roll(top, P_COV, 1), pltpu.roll(bottom, P_COV, 1)
         packed[i], packed[i + 1] = both[:P_COV], both[P_COV:]
@@ -379,7 +387,7 @@
             above = 16 * (i + 1)
             for k in (2 * w, 2 * w + 1):
                 gram_ref[i, pl.ds(k, above, N_BASIS), :] = turned[(k - 2 * w) * P_COV : (k - 2 * w) * P_COV + above, :]
-    moment = sums_ref[MOMENT_ROW : MOMENT_ROW + N_BASIS, 0:P_COV].T * (1.0 / math.sqrt(TOTAL_LIVE))
+    moment = small[8:16, 0:P_COV].T * (1.0 / math.sqrt(TOTAL_LIVE))
     for j in range(N_BASIS):
         gram_ref[4, pl.ds(j, P_COV, N_BASIS), :] = jnp.broadcast_to(moment[:, j : j + 1], (P_COV, 128))
 
@@ -438,17 +446,23 @@
 
 
 NEAR = ("zn", "yn", "core", "x")
-FAR = ("zf", "yf")
-
-
-def exchange(rows, axes, parts):
-    return lax.all_to_all(rows.reshape(parts, -1, 128), axes, 0, 0, tiled=True).reshape(-1, 128)
+FAR = ("zf", "zn", "yf", "yn")
+FAR_GROUPS = [
+    [((zf * 2 + (z ^ turn(zf))) * 4 + yf) * 2 + (y ^ turn(yf)) for zf in range(4) for yf in range(4)]
+    for z in range(2)
+    for y in range(2)
+]
+
+
+def exchange(rows, axes, parts, groups=None):
+    split = rows.reshape(parts, -1, 128)
+    return lax.all_to_all(split, axes, 0, 0, tiled=True, axis_index_groups=groups).reshape(-1, 128)
 
 
 def per_device(covariates, intervals, offsets, responses, counts, smoothing):
     sums = local_sums(counts, covariates, intervals, offsets, responses)
     shares = sum_repeat(exchange(sums, NEAR, SHARES), SHARES, 16)
-    shares = sum_repeat(exchange(shares, FAR, 16), 16, SHARES)
+    shares = sum_repeat(exchange(shares, FAR, 16, FAR_GROUPS), 16, SHARES)
     factor, projected = factorize(exchange(shares, NEAR, SHARES), smoothing)
     return factor, projected[0]
 

time: 78.9 us -> 77.3 us (0.980)
  blocking collectives: 58.6 us -> 53.6 us
  Pallas kernels: 18.7 us -> 22.1 us
    all_to_all x3, blocking collectives: 58.6 us -> 53.6 us  [exchange(): lax.all_to_all(split, axes, 0, 0, tiled=True, axis_index_groups=groups)]
    pallas_call x1, Pallas kernels: 5.63 us -> 9 us  [local_sums(): pl.pallas_call(gram_kernel, in_specs=[pl.BlockSpec(memory_space=pltpu.SME...]
where the time goes in v6:
time: 77.3 us; the launch traced here: 77 us
  blocking collectives  53.6 us (69%)
  Pallas kernels  22.1 us (29%)
  between operations  1.3 us (2%)
    all_to_all x3, blocking collectives, exchange(): lax.all_to_all(split, axes, 0, 0, tiled=True, axis_index_groups=groups)  53.6 us
    pallas_call x1, Pallas kernels, factorize(): pl.pallas_call(factor_kernel, out_shape=(jax.ShapeDtypeStruct((WIDTH, WID...  13 us
    pallas_call x1, Pallas kernels, local_sums(): pl.pallas_call(gram_kernel, in_specs=[pl.BlockSpec(memory_space=pltpu.SME...  9 us

profile of v6, /device:TPU:1, one launch (start us, length us, event | category | flops | bytes accessed | tf_op | source)
XLA Modules:
  0.0 77.0 jit_solution(9727914076851473909)
XLA Ops:
  1.3 0.0 copy-start
  1.3 9.0 %local_sums.1 = f32[512,128]{1,0:T(8,128)} custom-call(s32[1]{0:T(128)S(6)} %copy.8.count_ref, f32[64,8192]{1,0:T(8,128)} %cov_hbm.1, s32[1,8192]{1,0:T(1,128)} %bitcast.18, f32[1,8192]{1,0:T(1,128)} %bitcast.19, f32[1,8192]{1,0:T(1,128)} %bitcast.20), custom_call_target="tpu_custom_call" | custom-call | tf_op jit(solution)/shard_map/local_sums/pallas_call | solution.py:202
  10.3 16.2 %all_to_all.15 = f32[32,16,128]{2,1,0:T(8,128)S(1)} all-to-all(f32[32,16,128]{2,1,0:T(8,128)} %bitcast.17), channel_id=1, replica_groups=mesh['zf'=4,'zn'=2,'yf'=4,'yn'=2,'core'=2,'x'=4] {'zn','yn','core','x'}, dimensions={0} | all-to-all | bytes 524288 | tf_op jit(solution)/shard_map/all_to_all | solution.py:459
  26.6 23.2 %all_to_all.16 = f32[16,16,128]{2,1,0:T(8,128)S(1)} all-to-all(f32[16,16,128]{2,1,0:T(8,128)S(1)} %bitcast.14), channel_id=1, replica_groups={{72,80,96,120,136,144,160,184,264,272,288,312,456,464,480,504},{64,88,1..., dimensions={0} | all-to-all | bytes 262144 | tf_op jit(solution)/shard_map/all_to_all | solution.py:459
  49.8 14.2 %all_to_all.17 = f32[32,16,128]{2,1,0:T(8,128)S(1)} all-to-all(f32[32,16,128]{2,1,0:T(8,128)S(1)} %bitcast.13), channel_id=1, replica_groups=mesh['zf'=4,'zn'=2,'yf'=4,'yn'=2,'core'=2,'x'=4] {'zn','yn','core','x'}, dimensions={0} | all-to-all | bytes 524288 | tf_op jit(solution)/shard_map/all_to_all | solution.py:459
  64.0 0.0 copy-done
  64.0 13.0 %factorize.1 = (f32[512,512]{1,0:T(8,128)}, f32[1,512]{1,0:T(1,128)}) custom-call(f32[512,128]{1,0:T(8,128)S(1)} %bitcast.11, f32[1,64]{1,0:T(1,128)S(1)} %bitcast.16), custom_call_target="tpu_custom_call" | custom-call | tf_op jit(solution)/shard_map/factorize/pallas_call | solution.py:433
  (2 shorter events, 0.1 us)
Async XLA Ops:
  1.3 62.7 %copy-start = (f32[64]{0:T(128)S(1)}, f32[64]{0:T(128)}, u32[]{:S(2)}) copy-start(f32[64]{0:T(128)} %param.11) | copy-start | bytes 772

commit v7 on v6

--- a/solution.py
+++ b/solution.py
@@ -56,10 +56,9 @@
 
 
 def gram_kernel(
-    count_ref, cov_hbm, int_hbm, off_hbm, resp_hbm, out_ref,
-    cov_ref, int_ref, off_ref, resp_ref, hi_even, hi_odd, lo_even, lo_odd, mid_ref, end_ref, mom_ref, row_sem, cov_sem,
+    count_hbm, cov_hbm, int_hbm, off_hbm, resp_hbm, out_ref,
+    count_ref, cov_ref, int_ref, off_ref, resp_ref, hi_even, hi_odd, lo_even, lo_odd, mid_ref, end_ref, mom_ref, row_sem, cov_sem,
 ):
-    count = count_ref[0]
     chunks = cov_hbm.shape[1] // CHUNK
 
     def columns(c):
@@ -67,7 +66,9 @@
 
     row_copies = [
         pltpu.make_async_copy(source, target, row_sem.at[i])
-        for i, (source, target) in enumerate([(int_hbm, int_ref), (off_hbm, off_ref), (resp_hbm, resp_ref)])
+        for i, (source, target) in enumerate(
+            [(count_hbm, count_ref), (int_hbm, int_ref), (off_hbm, off_ref), (resp_hbm, resp_ref)]
+        )
     ]
     groups = chunks // UNROLL
 
@@ -84,6 +85,7 @@
     mom_ref[...] = jnp.zeros_like(mom_ref)
     for copy in row_copies:
         copy.wait()
+    count = count_ref[0, 0]
 
     def build(c, hi_ref, lo_ref):
         part = columns(c)
@@ -201,9 +203,10 @@
     low = pltpu.VMEM((WIDTH + len(LO_SUMS) * P_COV, CHUNK), BF16)
     return pl.pallas_call(
         gram_kernel,
-        in_specs=[pl.BlockSpec(memory_space=pltpu.SMEM), in_place, in_place, in_place, in_place],
+        in_specs=[in_place] * 5,
         out_shape=jax.ShapeDtypeStruct((SLAB_ROWS, 128), F32),
         scratch_shapes=[
+            pltpu.SMEM((1, 1), jnp.int32),
             pltpu.VMEM((P_COV, slots), F32),
             pltpu.VMEM((1, slots), jnp.int32),
             pltpu.VMEM((1, slots), F32),
@@ -215,12 +218,12 @@
             pltpu.VMEM((2 * len(MID_ROWS) * P_COV, 256), F32),
             pltpu.VMEM(((len(END_HI_ROWS) + len(END_LO_ROWS)) * P_COV, 256), F32),
             pltpu.VMEM((16, 128), F32),
-            pltpu.SemaphoreType.DMA((3,)),
+            pltpu.SemaphoreType.DMA((4,)),
             pltpu.SemaphoreType.DMA((slots // (UNROLL * CHUNK),)),
         ],
         compiler_params=pltpu.CompilerParams(vmem_limit_bytes=62 * 1024 * 1024),
         name="local_sums",
-    )(count, covariates, intervals[None, :], offsets[None, :], responses[None, :])
+    )(count[None, :], covariates, intervals[None, :], offsets[None, :], responses[None, :])
 
 
 def sum_repeat_kernel(parts, copies, in_ref, out_ref):

time: 77.3 us -> 77.1 us (level)
  Pallas kernels: 22.1 us -> 18.7 us
  blocking collectives: 53.6 us -> 56.6 us
    pallas_call x1, Pallas kernels: 9 us -> 5.64 us  [local_sums(): pl.pallas_call(gram_kernel, in_specs=[in_place] * 5, out_shape=jax.ShapeD...]
    all_to_all x3, blocking collectives: 53.6 us -> 56.6 us  [exchange(): lax.all_to_all(split, axes, 0, 0, tiled=True, axis_index_groups=groups)]
where the time goes in v7:
time: 77.1 us; the launch traced here: 76.6 us
  blocking collectives  56.6 us (73%)
  Pallas kernels  18.7 us (24%)
  between operations  1.3 us (2%)
    all_to_all x3, blocking collectives, exchange(): lax.all_to_all(split, axes, 0, 0, tiled=True, axis_index_groups=groups)  56.6 us
    pallas_call x1, Pallas kernels, factorize(): pl.pallas_call(factor_kernel, out_shape=(jax.ShapeDtypeStruct((WIDTH, WID...  13 us
    pallas_call x1, Pallas kernels, local_sums(): pl.pallas_call(gram_kernel, in_specs=[in_place] * 5, out_shape=jax.ShapeD...  5.64 us

profile of v7, /device:TPU:1, one launch (start us, length us, event | category | flops | bytes accessed | tf_op | source)
XLA Modules:
  0.0 76.6 jit_solution(12401186549455720217)
XLA Ops:
  1.3 0.0 copy-start
  1.3 5.6 %local_sums.1 = f32[512,128]{1,0:T(8,128)} custom-call(s32[1,1]{1,0:T(1,128)} %bitcast.12.count_hbm, f32[64,8192]{1,0:T(8,128)} %cov_hbm.1, s32[1,8192]{1,0:T(1,128)} %bitcast.20, f32[1,8192]{1,0:T(1,128)} %bitcast.21, f32[1,8192]{1,0:T(1,128)} %bitcast.22), custom_call_target="tpu_custom_call" | custom-call | tf_op jit(solution)/shard_map/local_sums/pallas_call | solution.py:204
  6.9 22.1 %all_to_all.15 = f32[32,16,128]{2,1,0:T(8,128)S(1)} all-to-all(f32[32,16,128]{2,1,0:T(8,128)} %bitcast.19), channel_id=1, replica_groups=mesh['zf'=4,'zn'=2,'yf'=4,'yn'=2,'core'=2,'x'=4] {'zn','yn','core','x'}, dimensions={0} | all-to-all | bytes 524288 | tf_op jit(solution)/shard_map/all_to_all | solution.py:462
  29.1 20.2 %all_to_all.16 = f32[16,16,128]{2,1,0:T(8,128)S(1)} all-to-all(f32[16,16,128]{2,1,0:T(8,128)S(1)} %bitcast.16), channel_id=1, replica_groups={{72,80,96,120,136,144,160,184,264,272,288,312,456,464,480,504},{64,88,1..., dimensions={0} | all-to-all | bytes 262144 | tf_op jit(solution)/shard_map/all_to_all | solution.py:462
  49.4 14.3 %all_to_all.17 = f32[32,16,128]{2,1,0:T(8,128)S(1)} all-to-all(f32[32,16,128]{2,1,0:T(8,128)S(1)} %bitcast.15), channel_id=1, replica_groups=mesh['zf'=4,'zn'=2,'yf'=4,'yn'=2,'core'=2,'x'=4] {'zn','yn','core','x'}, dimensions={0} | all-to-all | bytes 524288 | tf_op jit(solution)/shard_map/all_to_all | solution.py:462
  63.6 0.0 copy-done
  63.7 13.0 %factorize.1 = (f32[512,512]{1,0:T(8,128)}, f32[1,512]{1,0:T(1,128)}) custom-call(f32[512,128]{1,0:T(8,128)S(1)} %bitcast.13, f32[1,64]{1,0:T(1,128)S(1)} %bitcast.18), custom_call_target="tpu_custom_call" | custom-call | tf_op jit(solution)/shard_map/factorize/pallas_call | solution.py:436
  (2 shorter events, 0.1 us)
Async XLA Ops:
  1.3 62.4 %copy-start = (f32[64]{0:T(128)S(1)}, f32[64]{0:T(128)}, u32[]{:S(2)}) copy-start(f32[64]{0:T(128)} %param.11) | copy-start | bytes 772

commit v8 on v7

--- a/solution.py
+++ b/solution.py
@@ -450,8 +450,9 @@
 
 NEAR = ("zn", "yn", "core", "x")
 FAR = ("zf", "zn", "yf", "yn")
+FAR_ORDER = [divmod(9 * i % 16, 4) for i in range(16)]
 FAR_GROUPS = [
-    [((zf * 2 + (z ^ turn(zf))) * 4 + yf) * 2 + (y ^ turn(yf)) for zf in range(4) for yf in range(4)]
+    [((zf * 2 + (z ^ turn(zf))) * 4 + yf) * 2 + (y ^ turn(yf)) for zf, yf in FAR_ORDER]
     for z in range(2)
     for y in range(2)
 ]

time: 77.1 us -> 77.2 us (level)
  no operation moved by 1% of the time
where the time goes in v8:
time: 77.2 us; the launch traced here: 77 us
  blocking collectives  57 us (74%)
  Pallas kernels  18.7 us (24%)
  between operations  1.3 us (2%)
    all_to_all x3, blocking collectives, exchange(): lax.all_to_all(split, axes, 0, 0, tiled=True, axis_index_groups=groups)  57 us
    pallas_call x1, Pallas kernels, factorize(): pl.pallas_call(factor_kernel, out_shape=(jax.ShapeDtypeStruct((WIDTH, WID...  13 us
    pallas_call x1, Pallas kernels, local_sums(): pl.pallas_call(gram_kernel, in_specs=[in_place] * 5, out_shape=jax.ShapeD...  5.64 us

profile of v8, /device:TPU:1, one launch (start us, length us, event | category | flops | bytes accessed | tf_op | source)
XLA Modules:
  0.0 77.0 jit_solution(1421085420318124147)
XLA Ops:
  1.3 0.0 copy-start
  1.3 5.6 %local_sums.1 = f32[512,128]{1,0:T(8,128)} custom-call(s32[1,1]{1,0:T(1,128)} %bitcast.12.count_hbm, f32[64,8192]{1,0:T(8,128)} %cov_hbm.1, s32[1,8192]{1,0:T(1,128)} %bitcast.20, f32[1,8192]{1,0:T(1,128)} %bitcast.21, f32[1,8192]{1,0:T(1,128)} %bitcast.22), custom_call_target="tpu_custom_call" | custom-call | tf_op jit(solution)/shard_map/local_sums/pallas_call | solution.py:204
  6.9 20.4 %all_to_all.15 = f32[32,16,128]{2,1,0:T(8,128)S(1)} all-to-all(f32[32,16,128]{2,1,0:T(8,128)} %bitcast.19), channel_id=1, replica_groups=mesh['zf'=4,'zn'=2,'yf'=4,'yn'=2,'core'=2,'x'=4] {'zn','yn','core','x'}, dimensions={0} | all-to-all | bytes 524288 | tf_op jit(solution)/shard_map/all_to_all | solution.py:463
  27.4 22.3 %all_to_all.16 = f32[16,16,128]{2,1,0:T(8,128)S(1)} all-to-all(f32[16,16,128]{2,1,0:T(8,128)S(1)} %bitcast.16), channel_id=1, replica_groups={{72,272,96,312,136,464,160,504,264,80,288,120,456,144,480,184},{64,280,..., dimensions={0} | all-to-all | bytes 262144 | tf_op jit(solution)/shard_map/all_to_all | solution.py:463
  49.8 14.3 %all_to_all.17 = f32[32,16,128]{2,1,0:T(8,128)S(1)} all-to-all(f32[32,16,128]{2,1,0:T(8,128)S(1)} %bitcast.15), channel_id=1, replica_groups=mesh['zf'=4,'zn'=2,'yf'=4,'yn'=2,'core'=2,'x'=4] {'zn','yn','core','x'}, dimensions={0} | all-to-all | bytes 524288 | tf_op jit(solution)/shard_map/all_to_all | solution.py:463
  64.0 0.0 copy-done
  64.0 13.0 %factorize.1 = (f32[512,512]{1,0:T(8,128)}, f32[1,512]{1,0:T(1,128)}) custom-call(f32[512,128]{1,0:T(8,128)S(1)} %bitcast.13, f32[1,64]{1,0:T(1,128)S(1)} %bitcast.18), custom_call_target="tpu_custom_call" | custom-call | tf_op jit(solution)/shard_map/factorize/pallas_call | solution.py:436
  (2 shorter events, 0.1 us)
Async XLA Ops:
  1.3 62.7 %copy-start = (f32[64]{0:T(128)S(1)}, f32[64]{0:T(128)}, u32[]{:S(2)}) copy-start(f32[64]{0:T(128)} %param.11) | copy-start | bytes 772
